TPU v7x, 32 devices: a whole 2x2x4 slice. The times are simulated.
32 devices in a mesh: lat: 4 (over y, x), grid: 8 (over z, core).
Axes of the slice: x: 2, y: 2, z: 4, core: 2. Of those that a mesh axis runs over, the one named last changes fastest.
Arguments:
- grid_state: bfloat16 [192, 1280, 4096], P(None, 'lat', 'grid'), may hold values from -6 to 6
- radiation: bfloat16 [192, 192], replicated, may hold values from -0.4375 to 0.4375
- cloud_slots: int32 [4, 8, 8, 512], P('lat', 'grid'), may hold values from 0 to 163840, as said below
- wave_order: int32 [640], replicated, may hold values from 0 to 639, each once
- legendre: bfloat16 [640, 1280, 640], P(('lat', 'grid')), may hold values from -0.15625 to 0.15625
Outputs:
- spectral: bfloat16 [640, 384, 640], P(('lat', 'grid'))
Inputs may be any that keep to these rules, and one draw needn't show every extreme that they name: cloud_slots[l, g, h, s] is a column index of device (l, g) among its 163840 columns, and helper h of the band is the one listed for it; the value 163840 marks an empty slot; no column is listed twice by one device. `wave_order`: each wavenumber stands in exactly one slot.
All inputs are finite; a program needn't handle non-finite values.
Results may differ from a plain program's by a relative error of at most 0.0058.
Values may be sent and summed in bfloat16 or wider, within the bound.
No kernel may reach another device: no remote copies, remote signals or barrier semaphores. Data moves between devices by JAX's collectives and lax.ppermute only.
A program may use at most 384 MiB of HBM per device.

v0:
```python
import math

import jax
import jax.numpy as jnp
from jax import lax
from jax.sharding import PartitionSpec as P


def cloud_heating(columns, radiation):
    blended = jnp.einsum("fsc,fg->gsc", columns, radiation, preferred_element_type=jnp.float32)
    return (2.0 * jnp.tanh(blended)).astype(jnp.bfloat16)


def fourier_table(wave_order, nlon):
    longitude = jnp.arange(nlon, dtype=jnp.int32)
    phases = wave_order[:, None] * longitude[None, :] % nlon
    angles = phases.astype(jnp.float32) * (2.0 * math.pi / nlon)
    return jnp.stack([jnp.cos(angles), -jnp.sin(angles)]).astype(jnp.bfloat16)


def on_device(grid_state, radiation, cloud_slots, wave_order, legendre):
    levels, band_rows, lon_width = grid_state.shape
    groups = lax.axis_size("grid")
    nlon = lon_width * groups
    columns = band_rows * lon_width
    flat_state = grid_state.reshape(levels, columns)
    slot_list = cloud_slots[0, 0]
    picked = jnp.take(flat_state, slot_list, axis=1, mode="fill", fill_value=0)
    heating = cloud_heating(picked, radiation)
    placed = (
        jnp.zeros_like(flat_state)
        .at[:, slot_list.reshape(-1)]
        .set(heating.reshape(levels, -1), mode="drop")
    )
    heated = (flat_state.astype(jnp.float32) + placed.astype(jnp.float32)).astype(jnp.bfloat16)
    lat_rows = lax.all_to_all(
        heated.reshape(levels, band_rows, lon_width),
        "grid",
        split_axis=1,
        concat_axis=2,
        tiled=True,
    )
    basis_table = fourier_table(wave_order, nlon)
    scaled = jnp.einsum(
        "rml,fjl->mjrf", basis_table, lat_rows, preferred_element_type=jnp.float32
    ) * (1.0 / math.sqrt(nlon))
    total_waves = scaled.shape[0]
    row_count = scaled.shape[1]
    coefs = scaled.reshape(total_waves, row_count, 2 * levels).astype(jnp.bfloat16)
    owned_count = legendre.shape[0]
    owned = lax.all_to_all(coefs, ("lat", "grid"), split_axis=0, concat_axis=1, tiled=True)
    position = lax.axis_index("lat") * groups + lax.axis_index("grid")
    mine = lax.dynamic_slice_in_dim(wave_order, position * owned_count, owned_count)
    spectra = jnp.einsum("kjc,kjn->kcn", owned, legendre, preferred_element_type=jnp.float32)
    degrees = jnp.arange(legendre.shape[2], dtype=jnp.int32)
    keep_mask = degrees[None, None, :] >= mine[:, None, None]
    return jnp.where(keep_mask, spectra, 0.0).astype(jnp.bfloat16)


def solution(mesh):
    in_specs = (
        P(None, "lat", "grid"),
        P(),
        P("lat", "grid", None, None),
        P(),
        P(("lat", "grid"), None, None),
    )
    out_specs = P(("lat", "grid"), None, None)
    return jax.shard_map(
        on_device, mesh=mesh, in_specs=in_specs, out_specs=out_specs, check_vma=False
    )
```

profile of v0, /device:TPU:0, one launch (start us, length us, event | category | flops | bytes accessed | tf_op | source)
XLA Modules:
  0.0 2650.1 jit_solution(9687126387922551231)
XLA Ops:
  0.0 0.0 copy-start
  0.0 0.8 fusion.29
  0.8 0.7 compare_and_fusion
  1.5 0.7 copy.38
  2.2 118.2 %copy.20 = bf16[192,320,512]{0,2,1:T(8,128)(2,1)} copy(bf16[192,320,512]{2,1,0:T(8,128)(2,1)} %param.5) | data formatting | bytes 125829120 | tf_op args[0]
  120.4 96.7 %gather_fusion = bf16[4096,192]{1,0:T(8,128)(2,1)S(1)} fusion(bf16[192,163840]{0,1:T(8,128)(2,1)} %bitcast, s32[4096]{0:T(1024)S(1)} %broadcast_clamp_fusion.1), kind=kCustom, calls=%fused_computation | custom fusion | bytes 3162112 | tf_op jit(solution)/shard_map/jit(_take)/gather | solution.py:28
  217.1 2.3 copy.21
  219.4 0.0 copy-done
  219.4 2.1 fusion.24
  221.5 0.2 copy.37
  221.6 2.5 copy.24
  224.1 5.1 sort
  229.3 98.5 %scatter_custom_fusion = bf16[192,163840]{0,1:T(8,128)(2,1)} fusion(s32[4096]{0:T(1024)S(1)} %get-tuple-element.5, bf16[]{:T(256)} %constant.29.clone.1, bf16[4096,192]{1,0:T(8,128)(2,1)} %copy.24, s32[4096]{0:T(1024)S(1)} %broadcast_clamp_fusion), kind=kCustom, calls=%fused_computation.6 | custom fusion | bytes 62915072 | tf_op jit(solution)/shard_map/scatter | solution.py:33
  327.8 79.4 %add_convert_fusion = bf16[192,163840]{0,1:T(8,128)(2,1)} fusion(bf16[192,163840]{0,1:T(8,128)(2,1)} %scatter_custom_fusion, bf16[192,320,512]{0,2,1:T(8,128)(2,1)} %copy.20), kind=kLoop, calls=%fused_computation.3 | loop fusion | flops 125829120 | bytes 188743680 | tf_op jit(solution)/shard_map/convert_element_type | solution.py:35
  407.3 89.5 %copy.25 = bf16[192,320,512]{2,0,1:T(8,128)(2,1)} copy(bf16[192,320,512]{0,2,1:T(8,128)(2,1)} %bitcast.9) | data formatting | bytes 125829120 | tf_op jit(solution)/shard_map/reshape | solution.py:37
  496.7 0.0 copy-start.2
  496.7 39.8 %all-to-all-start = ((bf16[192,320,512]{2,0,1:T(8,128)(2,1)}), bf16[192,320,512]{2,0,1:T(8,128)(2,1)}, u32[]{:S(2)}, u32[]{:S(2)}) async-start(bf16[192,320,512]{2,0,1:T(8,128)(2,1)} %copy.25), calls=%async_computation | async-start | bytes 125829120 | tf_op jit(solution)/shard_map/all_to_all | solution.py:36
  536.6 0.0 copy-done.2
  536.6 44.1 %cosine_convert_fusion = (bf16[1,640,4096]{2,1,0:T(8,128)(2,1)}, bf16[1,640,4096]{2,1,0:T(8,128)(2,1)}) fusion(s32[640]{0:T(1024)S(1)} %copy-done.2), kind=kLoop, calls=%fused_computation.21 | loop fusion | flops 44564480 | bytes 10488320 | tf_op jit(solution)/shard_map/convert
  580.7 1308.3 %all-to-all-done = bf16[192,320,512]{2,0,1:T(8,128)(2,1)} async-done(((bf16[192,320,512]{2,0,1:T(8,128)(2,1)}), bf16[192,320,512]{2,0,1:T(8,128)(2,1)}, u32[]{:S(2)}, u32[]{:S(2)}) %all-to-all-start) | async-done | bytes 62914592 | tf_op jit(solution)/shard_map/all_to_all | solution.py:36
  1889.0 56.2 %copy.27 = bf16[192,40,8,512]{3,2,1,0:T(8,128)(2,1)} copy(bf16[192,40,8,512]{3,0,1,2:T(8,128)(2,1)} %bitcast.12) | data formatting | bytes 125829120 | tf_op jit(solution)/shard_map/all_to_all | solution.py:36
  1945.1 92.3 %reshape.211 = bf16[192,40,4096,1]{2,1,0,3:T(8,128)(2,1)} reshape(bf16[192,40,8,512]{3,2,1,0:T(8,128)(2,1)} %copy.27) | data formatting | bytes 125829120 | tf_op jit(solution)/shard_map/all_to_all | solution.py:36
  2037.4 90.5 %fusion.7 = bf16[640,40,2,192]{0,1,2,3:T(8,128)(2,1)} fusion(bf16[192,40,4096,1]{2,1,0,3:T(8,128)(2,1)} %reshape.211, bf16[1,640,4096]{2,1,0:T(8,128)(2,1)} %get-tuple-element.8, bf16[1,640,4096]{2,1,0:T(8,128)(2,1)} %get-tuple-element.7), kind=kOutput, calls=%fused_computation.13 | convolution fusion | flops 80571269120 | bytes 93061120 | tf_op jit(solution)/shard_map/rml,fjl->mjrf/dot_general | solution.py:44
  2127.9 18.7 copy.28
  2146.6 25.7 copy.29
  2172.4 9.3 all-to-all-start.1
  2181.7 0.8 dynamic_slice.3
  2182.5 0.1 iota_compare_fusion
  2182.6 425.6 %all-to-all-done.1 = bf16[640,40,384]{2,1,0:T(8,128)(2,1)} async-done(((bf16[640,40,384]{2,1,0:T(8,128)(2,1)}), bf16[640,40,384]{2,1,0:T(8,128)(2,1)}, u32[]{:S(2)}, u32[]{:S(2)}) %all-to-all-start.1) | async-done | bytes 19660832 | tf_op jit(solution)/shard_map/all_to_all | solution.py:51
  2608.2 16.7 copy.30
  2624.9 0.0 copy-start.1
  2624.9 25.0 select_convert_fusion
  2649.8 0.0 copy-done.1
  (5 shorter events, 0.0 us)
Async XLA Ops:
  0.0 219.4 %copy-start = (bf16[192,192]{1,0:T(8,128)(2,1)S(1)}, bf16[192,192]{1,0:T(8,128)(2,1)}, u32[]{:S(2)}) copy-start(bf16[192,192]{1,0:T(8,128)(2,1)} %param.6) | copy-start | bytes 221188
  496.7 39.8 %copy-start.2 = (s32[640]{0:T(1024)S(1)}, s32[640]{0:T(1024)}, u32[]{:S(2)}) copy-start(s32[640]{0:T(1024)} %param.8) | copy-start | bytes 7684
  496.7 1392.2 %all-to-all-start = ((bf16[192,320,512]{2,0,1:T(8,128)(2,1)}), bf16[192,320,512]{2,0,1:T(8,128)(2,1)}, u32[]{:S(2)}, u32[]{:S(2)}) async-start(bf16[192,320,512]{2,0,1:T(8,128)(2,1)} %copy.25), calls=%async_computation | async-start | bytes 125829120 | tf_op jit(solution)/shard_map/all_to_all | solution.py:36
  2172.4 435.8 %all-to-all-start.1 = ((bf16[640,40,384]{2,1,0:T(8,128)(2,1)}), bf16[640,40,384]{2,1,0:T(8,128)(2,1)}, u32[]{:S(2)}, u32[]{:S(2)}) async-start(bf16[640,40,384]{2,1,0:T(8,128)(2,1)} %copy.29), calls=%async_computation.1 | async-start | bytes 39321600 | tf_op jit(solution)/shard_map/all_to_all | solution.py:51
  2624.9 25.0 copy-start.1
where the time goes:
time: 2670 us; the launch traced here: 2650 us
  waiting for transfers between devices  1730 us (65%)
  local copies, waits for them, and re-layouts  619 us (23%)
  other arithmetic  130 us (5%)
  matrix products  118 us (4%)
  starting transfers between devices  49.1 us (2%)
    all_to_all x1, waiting for transfers between devices, on_device(): lax.all_to_all(heated.reshape(levels, band_rows, lon_width), 'grid', spli...  1310 us
    all_to_all x1, waiting for transfers between devices, on_device(): lax.all_to_all(coefs, ('lat', 'grid'), split_axis=0, concat_axis=1, tiled...  426 us
    all_to_all x2, local copies, waits for them, and re-layouts, on_device(): lax.all_to_all(heated.reshape(levels, band_rows, lon_width), 'grid', spli...  148 us
    unnamed x9, local copies, waits for them, and re-layouts  119 us
    gather x2, local copies, waits for them, and re-layouts, on_device(): picked = jnp.take(flat_state, slot_list, axis=1, mode='fill', fill_value=0)  99 us
    scatter x2, local copies, waits for them, and re-layouts, on_device(): placed = jnp.zeros_like(flat_state).at[:, slot_list.reshape(-1)].set(heat...  98.6 us
    dot_general x1, matrix products, on_device(): jnp.einsum('rml,fjl->mjrf', basis_table, lat_rows, preferred_element_type...  90.5 us
    reshape x1, local copies, waits for them, and re-layouts, on_device(): heated.reshape(levels, band_rows, lon_width)  89.5 us
  transfers between devices with their start and end apart: 2, of which 2 were waited for; matrix products, arithmetic and copies ran while one was open for 2% of the time, Pallas kernels for 0%

commit v1 on v0

v1 whole, which is shorter than its diff:
```python
import math

import jax
import jax.numpy as jnp
import numpy as np
from jax import lax
from jax.sharding import PartitionSpec as P

SPARE = 24


def prolate_basis(width, waves, nlon):
    count = min(width, -(-2 * waves * width // nlon) + SPARE)
    band = (waves - 0.5) / nlon
    steps = np.arange(width, dtype=np.float64)
    centre = ((width - 1) / 2.0 - steps) ** 2 * np.cos(2.0 * np.pi * band)
    beside = steps[1:] * (width - steps[1:]) / 2.0
    system = np.diag(centre) + np.diag(beside, 1) + np.diag(beside, -1)
    _, vectors = np.linalg.eigh(system)
    leading = vectors[:, ::-1][:, :count]
    lead_sign = np.sign(np.sum(leading * (steps[:, None] + 1.0), axis=0))
    flat_sign = np.sign(np.sum(leading, axis=0))
    even = np.abs(np.sum(leading * leading[::-1], axis=0) - 1.0) < 1e-6
    return leading * np.where(even, np.where(flat_sign == 0, 1, flat_sign), np.where(lead_sign == 0, 1, lead_sign))


def fourier_table(wave_order, nlon):
    longitude = jnp.arange(nlon, dtype=jnp.int32)
    phases = wave_order[:, None] * longitude[None, :] % nlon
    angles = phases.astype(jnp.float32) * (2.0 * math.pi / nlon)
    return jnp.stack([jnp.cos(angles), -jnp.sin(angles)]).astype(jnp.bfloat16)


def cloud_mask(slots, band_rows, lon_width):
    slots = slots.reshape(-1)
    rows = (slots // lon_width)[None, :] == jnp.arange(band_rows, dtype=jnp.int32)[:, None]
    lons = (slots % lon_width)[:, None] == jnp.arange(lon_width, dtype=jnp.int32)[None, :]
    return jnp.dot(
        rows.astype(jnp.bfloat16), lons.astype(jnp.bfloat16), preferred_element_type=jnp.float32
    )


def on_device(grid_state, radiation, cloud_slots, wave_order, legendre):
    levels, band_rows, lon_width = grid_state.shape
    groups = lax.axis_size("grid")
    bands = lax.axis_size("lat")
    waves = wave_order.shape[0]
    nlon = lon_width * groups
    own_rows = band_rows // groups
    chunks = 5 if own_rows % 5 == 0 else 1
    chunk_rows = own_rows // chunks

    exact = prolate_basis(lon_width, waves, nlon)
    rank = exact.shape[1]
    compress = exact.astype(jnp.bfloat16)
    spread = exact @ np.linalg.inv(compress.astype(np.float64).T @ exact)

    mask = cloud_mask(cloud_slots, band_rows, lon_width).reshape(
        groups, own_rows, lon_width
    )
    state = grid_state.reshape(levels, groups, own_rows, lon_width)
    basis = fourier_table(wave_order, nlon).reshape(2, waves, groups, lon_width)
    expand = jnp.einsum(
        "rkgl,ln->krgn",
        basis.astype(jnp.float32),
        jnp.asarray(spread, jnp.float32),
        precision=lax.Precision.HIGHEST,
    )
    expand = (expand * (1.0 / math.sqrt(nlon))).astype(jnp.bfloat16)
    expand = expand.reshape(2 * waves, groups * rank)

    arrived = []
    for part in range(chunks):
        first = part * chunk_rows
        piece = state[:, :, first : first + chunk_rows]
        flag = mask[:, first : first + chunk_rows]
        blended = jnp.einsum("fgjl,fh->gjhl", piece, radiation, preferred_element_type=jnp.float32)
        heating = (2.0 * jnp.tanh(blended)).astype(jnp.bfloat16).astype(jnp.float32)
        heated = piece.transpose(1, 2, 0, 3).astype(jnp.float32) + heating * flag[:, :, None, :]
        packed = jnp.einsum(
            "gjhl,ln->gnjh",
            heated.astype(jnp.bfloat16),
            jnp.asarray(compress),
            preferred_element_type=jnp.float32,
        ).astype(jnp.bfloat16)
        packed = packed.reshape(groups * rank, chunk_rows * levels)
        rows = lax.all_to_all(packed, "grid", split_axis=0, concat_axis=0, tiled=True)
        coefs = jnp.dot(expand, rows, preferred_element_type=jnp.float32).astype(jnp.bfloat16)
        coefs = coefs.reshape(waves, 2, chunk_rows, levels).transpose(0, 2, 1, 3)
        coefs = coefs.reshape(waves, chunk_rows, 2 * levels)
        owned = lax.all_to_all(coefs, ("lat", "grid"), split_axis=0, concat_axis=0, tiled=True)
        arrived.append(owned.reshape(bands * groups, -1, chunk_rows, 2 * levels))

    owned_count = legendre.shape[0]
    owned = jnp.stack(arrived, axis=2).transpose(1, 0, 2, 3, 4)
    owned = owned.reshape(owned_count, bands * groups * own_rows, 2 * levels)
    position = lax.axis_index("lat") * groups + lax.axis_index("grid")
    mine = lax.dynamic_slice_in_dim(wave_order, position * owned_count, owned_count)
    spectra = jnp.einsum("kjc,kjn->kcn", owned, legendre, preferred_element_type=jnp.float32)
    degrees = jnp.arange(legendre.shape[2], dtype=jnp.int32)
    keep_mask = degrees[None, None, :] >= mine[:, None, None]
    return jnp.where(keep_mask, spectra, 0.0).astype(jnp.bfloat16)


def solution(mesh):
    in_specs = (
        P(None, "lat", "grid"),
        P(),
        P("lat", "grid", None, None),
        P(),
        P(("lat", "grid"), None, None),
    )
    out_specs = P(("lat", "grid"), None, None)
    return jax.shard_map(
        on_device, mesh=mesh, in_specs=in_specs, out_specs=out_specs, check_vma=False
    )
```

time: 2670 us -> 1160 us (0.43)
  waiting for transfers between devices: 1730 us -> 568 us
  local copies, waits for them, and re-layouts: 619 us -> 317 us
  other arithmetic: 130 us -> 42.7 us
  matrix products: 118 us -> 170 us
    all_to_all x2 -> x10, waiting for transfers between devices: 1730 us -> 568 us  [the longest x5 291 us: on_device(): lax.all_to_all(coefs, ('lat', 'grid'), split_axis=0, concat_axis=0, tiled...]
    all_to_all x3 -> x5, local copies, waits for them, and re-layouts: 165 us -> 50.3 us  [on_device(): lax.all_to_all(packed, 'grid', split_axis=0, concat_axis=0, tiled=True)]
    gather x2 -> x0, local copies, waits for them, and re-layouts: 99 us -> none  [on_device(): picked = jnp.take(flat_state, slot_list, axis=1, mode='fill', fill_value=0)]
    scatter x2 -> x0, local copies, waits for them, and re-layouts: 98.6 us -> none  [on_device(): placed = jnp.zeros_like(flat_state).at[:, slot_list.reshape(-1)].set(heat...]
    convert_element_type x1 -> x0, other arithmetic: 79.4 us -> none  [on_device(): (flat_state.astype(jnp.float32) + placed.astype(jnp.float32)).astype(jnp....]
    transpose x0 -> x6, local copies, waits for them, and re-layouts: none -> 58.8 us  [the longest x5 42 us: on_device(): coefs = coefs.reshape(waves, 2, chunk_rows, levels).transpose(0, 2, 1, 3)]
    dot_general x2 -> x12, matrix products: 92.6 us -> 145 us  [the longest x5 75.9 us: on_device(): jnp.einsum('gjhl,ln->gnjh', heated.astype(jnp.bfloat16), jnp.asarray(comp...]
    unnamed x9 -> x16, local copies, waits for them, and re-layouts: 119 us -> 74.6 us
  transfers between devices with their start and end apart: 2 -> 10, of which waited for: 2 -> 9; matrix products, arithmetic and copies ran while one was open for 2% -> 31% of each run, Pallas kernels for 0% -> 0%
where the time goes in v1:
time: 1160 us; the launch traced here: 1140 us
  waiting for transfers between devices  568 us (49%)
  local copies, waits for them, and re-layouts  317 us (27%)
  matrix products  170 us (15%)
  starting transfers between devices  47 us (4%)
  other arithmetic  42.7 us (4%)
    all_to_all x5, waiting for transfers between devices, on_device(): lax.all_to_all(coefs, ('lat', 'grid'), split_axis=0, concat_axis=0, tiled...  291 us
    all_to_all x5, waiting for transfers between devices, on_device(): lax.all_to_all(packed, 'grid', split_axis=0, concat_axis=0, tiled=True)  277 us
    dot_general x5, matrix products, on_device(): jnp.einsum('gjhl,ln->gnjh', heated.astype(jnp.bfloat16), jnp.asarray(comp...  75.9 us
    unnamed x16, local copies, waits for them, and re-layouts  74.6 us
    dot_general x5, matrix products, on_device(): jnp.dot(expand, rows, preferred_element_type=jnp.float32)  53.4 us
    all_to_all x5, local copies, waits for them, and re-layouts, on_device(): lax.all_to_all(packed, 'grid', split_axis=0, concat_axis=0, tiled=True)  50.3 us
    reshape x5, local copies, waits for them, and re-layouts, on_device(): coefs = coefs.reshape(waves, 2, chunk_rows, levels).transpose(0, 2, 1, 3)  45.1 us
    another operation x1, other arithmetic  42.6 us
  transfers between devices with their start and end apart: 10, of which 9 were waited for; matrix products, arithmetic and copies ran while one was open for 31% of the time, Pallas kernels for 0%

profile of v1, /device:TPU:0, one launch (start us, length us, event | category | flops | bytes accessed | tf_op | source)
XLA Modules:
  0.0 1144.6 jit_solution(3765252502259567997)
XLA Ops:
  3.0 56.2 %copy.37 = bf16[192,320,512]{2,0,1:T(8,128)(2,1)} copy(bf16[192,320,512]{2,1,0:T(8,128)(2,1)} %param.7) | data formatting | bytes 125829120 | tf_op args[0]
  59.2 15.2 %convert_bitcast_fusion = bf16[8,184,8,192]{3,1,2,0:T(8,128)(2,1)} fusion(bf16[512,184,1,1]{0,1,3,2:T(8,128)(2,1)S(1)} %copy-done.4, f32[8,8,512]{2,1,0:T(8,128)S(1)} %get-tuple-element.5, bf16[192,8,40,512]{3,0,2,1:T(8,128)(2,1)} %bitcast.119, bf16[192,192]{1,0:T(8,128)(2,1)S(1)} %copy-done), kind=kOutput, calls=%fused_computation.68 | convolution fusion | flops 4777476096 | bytes 30081024 | tf_op jit(solution)/shard_map/gjhl,ln->gnjh/dot_general | solution.py:80
  74.4 6.5 copy.55
  80.9 10.1 all_to_all.71
  91.0 6.5 all-to-all-start.8
  97.5 15.3 %convert_bitcast_fusion.1 = bf16[8,184,8,192]{3,1,2,0:T(8,128)(2,1)} fusion(bf16[512,184,1,1]{0,1,3,2:T(8,128)(2,1)S(1)} %copy-done.4, f32[8,8,512]{2,1,0:T(8,128)S(1)} %get-tuple-element.6, bf16[192,8,40,512]{3,0,2,1:T(8,128)(2,1)} %bitcast.120, bf16[192,192]{1,0:T(8,128)(2,1)S(1)} %copy-done), kind=kOutput, calls=%fused_computation.69 | convolution fusion | flops 4777476096 | bytes 30081024 | tf_op jit(solution)/shard_map/gjhl,ln->gnjh/dot_general | solution.py:80
  112.8 6.5 copy.51
  119.3 10.1 all_to_all.67
  129.3 69.3 %all-to-all-done.8 = bf16[8,184,1536]{2,1,0:T(8,128)(2,1)} async-done(((bf16[8,184,1536]{2,1,0:T(8,128)(2,1)}), bf16[8,184,1536]{2,1,0:T(8,128)(2,1)}, u32[]{:S(2)}, u32[]{:S(2)}) %all-to-all-start.8) | async-done | bytes 4522016 | tf_op jit(solution)/shard_map/all_to_all | solution.py:87
  198.6 4.8 all-to-all-start.6
  203.4 15.2 %convert_bitcast_fusion.2 = bf16[8,184,8,192]{3,1,2,0:T(8,128)(2,1)} fusion(bf16[512,184,1,1]{0,1,3,2:T(8,128)(2,1)S(1)} %copy-done.4, f32[8,8,512]{2,1,0:T(8,128)S(1)} %get-tuple-element.7, bf16[192,8,40,512]{3,0,2,1:T(8,128)(2,1)} %bitcast.121, bf16[192,192]{1,0:T(8,128)(2,1)S(1)} %copy-done), kind=kOutput, calls=%fused_computation.70 | convolution fusion | flops 4777476096 | bytes 30081024 | tf_op jit(solution)/shard_map/gjhl,ln->gnjh/dot_general | solution.py:80
  218.6 6.5 copy.47
  225.1 10.0 all_to_all.63
  235.1 69.3 %all-to-all-done.6 = bf16[8,184,1536]{2,1,0:T(8,128)(2,1)} async-done(((bf16[8,184,1536]{2,1,0:T(8,128)(2,1)}), bf16[8,184,1536]{2,1,0:T(8,128)(2,1)}, u32[]{:S(2)}, u32[]{:S(2)}) %all-to-all-start.6) | async-done | bytes 4522016 | tf_op jit(solution)/shard_map/all_to_all | solution.py:87
  304.4 4.8 all-to-all-start.4
  309.3 15.2 %convert_bitcast_fusion.3 = bf16[8,184,8,192]{3,1,2,0:T(8,128)(2,1)} fusion(bf16[512,184,1,1]{0,1,3,2:T(8,128)(2,1)S(1)} %copy-done.4, f32[8,8,512]{2,1,0:T(8,128)S(1)} %get-tuple-element.8, bf16[192,8,40,512]{3,0,2,1:T(8,128)(2,1)} %bitcast.122, bf16[192,192]{1,0:T(8,128)(2,1)S(1)} %copy-done), kind=kOutput, calls=%fused_computation.71 | convolution fusion | flops 4777476096 | bytes 30081024 | tf_op jit(solution)/shard_map/gjhl,ln->gnjh/dot_general | solution.py:80
  324.5 6.5 copy.43
  331.0 10.0 all_to_all.59
  341.0 69.3 %all-to-all-done.4 = bf16[8,184,1536]{2,1,0:T(8,128)(2,1)} async-done(((bf16[8,184,1536]{2,1,0:T(8,128)(2,1)}), bf16[8,184,1536]{2,1,0:T(8,128)(2,1)}, u32[]{:S(2)}, u32[]{:S(2)}) %all-to-all-start.4) | async-done | bytes 4522016 | tf_op jit(solution)/shard_map/all_to_all | solution.py:87
  410.3 5.1 all-to-all-start.2
  415.4 15.1 %convert_bitcast_fusion.4 = bf16[8,184,8,192]{3,1,2,0:T(8,128)(2,1)} fusion(bf16[512,184,1,1]{0,1,3,2:T(8,128)(2,1)S(1)} %copy-done.4, f32[8,8,512]{2,1,0:T(8,128)S(1)} %get-tuple-element.9, bf16[192,8,40,512]{3,0,2,1:T(8,128)(2,1)} %bitcast.123, bf16[192,192]{1,0:T(8,128)(2,1)S(1)} %copy-done), kind=kOutput, calls=%fused_computation.72 | convolution fusion | flops 4777476096 | bytes 30081024 | tf_op jit(solution)/shard_map/gjhl,ln->gnjh/dot_general | solution.py:80
  430.5 6.6 copy.39
  437.0 10.1 all_to_all.55
  447.1 69.3 %all-to-all-done.2 = bf16[8,184,1536]{2,1,0:T(8,128)(2,1)} async-done(((bf16[8,184,1536]{2,1,0:T(8,128)(2,1)}), bf16[8,184,1536]{2,1,0:T(8,128)(2,1)}, u32[]{:S(2)}, u32[]{:S(2)}) %all-to-all-start.2) | async-done | bytes 4522016 | tf_op jit(solution)/shard_map/all_to_all | solution.py:87
  516.4 4.8 all-to-all-start
  521.2 42.6 %cosine_convert_fusion = (bf16[1,640,8,512]{3,1,2,0:T(8,128)(2,1)S(1)}, bf16[1,640,8,512]{3,1,2,0:T(8,128)(2,1)S(1)}) fusion(s32[8,512]{1,0:T(8,128)S(1)} %multiply_add_fusion, s32[640]{0:T(1024)S(1)} %copy-done.2), kind=kLoop, calls=%fused_computation.59 | loop fusion | flops 44564480 | bytes 10504704 | tf_op jit(solution)/shard_map/convert.10
  563.8 13.3 %fusion.69 = bf16[640,2,8,184]{0,3,2,1:T(8,128)(2,1)} fusion(f32[512,184,1,1]{0,1,3,2:T(8,128)S(1)} %copy-done.3, bf16[1,640,8,512]{3,1,2,0:T(8,128)(2,1)S(1)} %get-tuple-element.11, bf16[1,640,8,512]{3,1,2,0:T(8,128)(2,1)S(1)} %get-tuple-element.10), kind=kOutput, calls=%fused_computation.75 | convolution fusion | flops 11585290240 | bytes 14630912 | tf_op jit(solution)/shard_map/rkgl,ln->krgn/dot_general | solution.py:63
  577.1 8.4 copy.36
  585.5 9.6 reshape.225
  595.2 10.9 convolution_convert_fusion.1
  606.0 9.0 reshape.235
  615.0 8.4 copy.52
  623.5 6.6 copy.53
  630.0 6.2 all-to-all-start.7
  636.2 10.6 convolution_convert_fusion.2
  646.8 9.0 reshape.233
  655.8 8.4 copy.48
  664.2 6.6 copy.49
  670.8 54.9 %all-to-all-done.7 = bf16[640,8,384]{2,1,0:T(8,128)(2,1)} async-done(((bf16[640,8,384]{2,1,0:T(8,128)(2,1)}), bf16[640,8,384]{2,1,0:T(8,128)(2,1)}, u32[]{:S(2)}, u32[]{:S(2)}) %all-to-all-start.7) | async-done | bytes 3932192 | tf_op jit(solution)/shard_map/all_to_all | solution.py:91
  725.7 4.0 all-to-all-start.5
  729.6 10.7 convolution_convert_fusion.4
  740.3 9.0 reshape.229
  749.3 8.4 copy.40
  757.7 6.6 copy.41
  764.3 54.8 %all-to-all-done.5 = bf16[640,8,384]{2,1,0:T(8,128)(2,1)} async-done(((bf16[640,8,384]{2,1,0:T(8,128)(2,1)}), bf16[640,8,384]{2,1,0:T(8,128)(2,1)}, u32[]{:S(2)}, u32[]{:S(2)}) %all-to-all-start.5) | async-done | bytes 3932192 | tf_op jit(solution)/shard_map/all_to_all | solution.py:91
  822.6 10.6 convolution_convert_fusion.3
  833.2 9.0 reshape.231
  842.3 8.4 copy.44
  850.7 6.6 copy.45
  857.2 54.9 %all-to-all-done.1 = bf16[640,8,384]{2,1,0:T(8,128)(2,1)} async-done(((bf16[640,8,384]{2,1,0:T(8,128)(2,1)}), bf16[640,8,384]{2,1,0:T(8,128)(2,1)}, u32[]{:S(2)}, u32[]{:S(2)}) %all-to-all-start.1) | async-done | bytes 3932192 | tf_op jit(solution)/shard_map/all_to_all | solution.py:91
  912.1 3.7 all-to-all-start.3
  915.8 10.7 convolution_convert_fusion
  926.5 9.0 reshape.237
  935.5 8.4 copy.56
  943.9 6.6 copy.57
  950.5 54.8 %all-to-all-done.3 = bf16[640,8,384]{2,1,0:T(8,128)(2,1)} async-done(((bf16[640,8,384]{2,1,0:T(8,128)(2,1)}), bf16[640,8,384]{2,1,0:T(8,128)(2,1)}, u32[]{:S(2)}, u32[]{:S(2)}) %all-to-all-start.3) | async-done | bytes 3932192 | tf_op jit(solution)/shard_map/all_to_all | solution.py:91
  1009.0 4.4 constant_dynamic-update-slice_fusion.4
  1013.4 4.4 constant_dynamic-update-slice_fusion.3
  1017.8 4.4 constant_dynamic-update-slice_fusion.2
  1022.2 4.4 constant_dynamic-update-slice_fusion.1
  1026.6 71.7 %all-to-all-done.9 = bf16[640,8,384]{2,1,0:T(8,128)(2,1)} async-done(((bf16[640,8,384]{2,1,0:T(8,128)(2,1)}), bf16[640,8,384]{2,1,0:T(8,128)(2,1)}, u32[]{:S(2)}, u32[]{:S(2)}) %all-to-all-start.9) | async-done | bytes 3932192 | tf_op jit(solution)/shard_map/all_to_all | solution.py:91
  1098.3 4.4 constant_dynamic-update-slice_fusion
  1102.7 16.8 %copy.58 = bf16[20,32,5,8,384]{4,3,2,1,0:T(8,128)(2,1)} copy(bf16[20,32,5,8,384]{4,3,0,1,2:T(8,128)(2,1)} %bitcast.43) | data formatting | bytes 39321600 | tf_op jit(solution)/shard_map/transpose | solution.py:95
  1119.4 25.0 %select_convert_fusion = bf16[20,384,640]{2,1,0:T(8,128)(2,1)} fusion(pred[20,640]{1,0:T(8,128)(4,1)S(1)} %iota_compare_fusion.4, bf16[20,1280,384]{2,1,0:T(8,128)(2,1)} %bitcast.129, bf16[20,1280,640]{2,1,0:T(8,128)(2,1)} %param.11), kind=kOutput, calls=%fused_computation.13 | convolution fusion | flops 12592742400 | bytes 62272000 | tf_op jit(solution)/shard_map/kjc,kjn->kcn/dot_general | solution.py:99
  (20 shorter events, 10.3 us)
Async XLA Ops:
  0.0 59.2 %copy-start = (bf16[192,192]{1,0:T(8,128)(2,1)S(1)}, bf16[192,192]{1,0:T(8,128)(2,1)}, u32[]{:S(2)}) copy-start(bf16[192,192]{1,0:T(8,128)(2,1)} %param.8) | copy-start | bytes 221188
  3.0 56.2 %copy-start.4 = (bf16[512,184,1,1]{0,1,3,2:T(8,128)(2,1)S(1)}, bf16[512,184,1,1]{0,1,3,2:T(8,128)(2,1)}, u32[]{:S(2)}) copy-start(bf16[512,184,1,1]{0,1,3,2:T(8,128)(2,1)} %constant.76) | copy-start | bytes 565252
  91.0 107.6 %all-to-all-start.8 = ((bf16[8,184,1536]{2,1,0:T(8,128)(2,1)}), bf16[8,184,1536]{2,1,0:T(8,128)(2,1)}, u32[]{:S(2)}, u32[]{:S(2)}) async-start(bf16[8,184,1536]{2,1,0:T(8,128)(2,1)} %all_to_all.71), calls=%async_computation.8 | async-start | bytes 9043968 | tf_op jit(solution)/shard_map/all_to_all | solution.py:87
  198.6 105.8 %all-to-all-start.6 = ((bf16[8,184,1536]{2,1,0:T(8,128)(2,1)}), bf16[8,184,1536]{2,1,0:T(8,128)(2,1)}, u32[]{:S(2)}, u32[]{:S(2)}) async-start(bf16[8,184,1536]{2,1,0:T(8,128)(2,1)} %all_to_all.67), calls=%async_computation.6 | async-start | bytes 9043968 | tf_op jit(solution)/shard_map/all_to_all | solution.py:87
  304.4 105.9 %all-to-all-start.4 = ((bf16[8,184,1536]{2,1,0:T(8,128)(2,1)}), bf16[8,184,1536]{2,1,0:T(8,128)(2,1)}, u32[]{:S(2)}, u32[]{:S(2)}) async-start(bf16[8,184,1536]{2,1,0:T(8,128)(2,1)} %all_to_all.63), calls=%async_computation.4 | async-start | bytes 9043968 | tf_op jit(solution)/shard_map/all_to_all | solution.py:87
  410.3 106.1 %all-to-all-start.2 = ((bf16[8,184,1536]{2,1,0:T(8,128)(2,1)}), bf16[8,184,1536]{2,1,0:T(8,128)(2,1)}, u32[]{:S(2)}, u32[]{:S(2)}) async-start(bf16[8,184,1536]{2,1,0:T(8,128)(2,1)} %all_to_all.59), calls=%async_computation.2 | async-start | bytes 9043968 | tf_op jit(solution)/shard_map/all_to_all | solution.py:87
  437.0 84.2 %copy-start.2 = (s32[640]{0:T(1024)S(1)}, s32[640]{0:T(1024)}, u32[]{:S(2)}) copy-start(s32[640]{0:T(1024)} %param.10) | copy-start | bytes 7684
  447.1 116.7 %copy-start.3 = (f32[512,184,1,1]{0,1,3,2:T(8,128)S(1)}, f32[512,184,1,1]{0,1,3,2:T(8,128)}, u32[]{:S(2)}) copy-start(f32[512,184,1,1]{0,1,3,2:T(8,128)} %constant.75) | copy-start | bytes 1130500
  516.4 113.6 %all-to-all-start = ((bf16[8,184,1536]{2,1,0:T(8,128)(2,1)}), bf16[8,184,1536]{2,1,0:T(8,128)(2,1)}, u32[]{:S(2)}, u32[]{:S(2)}) async-start(bf16[8,184,1536]{2,1,0:T(8,128)(2,1)} %all_to_all.55), calls=%async_computation | async-start | bytes 9043968 | tf_op jit(solution)/shard_map/all_to_all | solution.py:87
  630.0 95.6 %all-to-all-start.7 = ((bf16[640,8,384]{2,1,0:T(8,128)(2,1)}), bf16[640,8,384]{2,1,0:T(8,128)(2,1)}, u32[]{:S(2)}, u32[]{:S(2)}) async-start(bf16[640,8,384]{2,1,0:T(8,128)(2,1)} %copy.53), calls=%async_computation.7 | async-start | bytes 7864320 | tf_op jit(solution)/shard_map/all_to_all | solution.py:91
  725.7 93.4 %all-to-all-start.5 = ((bf16[640,8,384]{2,1,0:T(8,128)(2,1)}), bf16[640,8,384]{2,1,0:T(8,128)(2,1)}, u32[]{:S(2)}, u32[]{:S(2)}) async-start(bf16[640,8,384]{2,1,0:T(8,128)(2,1)} %copy.49), calls=%async_computation.5 | async-start | bytes 7864320 | tf_op jit(solution)/shard_map/all_to_all | solution.py:91
  819.1 93.0 %all-to-all-start.1 = ((bf16[640,8,384]{2,1,0:T(8,128)(2,1)}), bf16[640,8,384]{2,1,0:T(8,128)(2,1)}, u32[]{:S(2)}, u32[]{:S(2)}) async-start(bf16[640,8,384]{2,1,0:T(8,128)(2,1)} %copy.41), calls=%async_computation.1 | async-start | bytes 7864320 | tf_op jit(solution)/shard_map/all_to_all | solution.py:91
  912.1 93.2 %all-to-all-start.3 = ((bf16[640,8,384]{2,1,0:T(8,128)(2,1)}), bf16[640,8,384]{2,1,0:T(8,128)(2,1)}, u32[]{:S(2)}, u32[]{:S(2)}) async-start(bf16[640,8,384]{2,1,0:T(8,128)(2,1)} %copy.45), calls=%async_computation.3 | async-start | bytes 7864320 | tf_op jit(solution)/shard_map/all_to_all | solution.py:91
  1005.3 93.0 %all-to-all-start.9 = ((bf16[640,8,384]{2,1,0:T(8,128)(2,1)}), bf16[640,8,384]{2,1,0:T(8,128)(2,1)}, u32[]{:S(2)}, u32[]{:S(2)}) async-start(bf16[640,8,384]{2,1,0:T(8,128)(2,1)} %copy.57), calls=%async_computation.9 | async-start | bytes 7864320 | tf_op jit(solution)/shard_map/all_to_all | solution.py:91
  1119.4 25.0 %copy-start.1 = (bf16[192,192]{1,0:T(8,128)(2,1)S(1)}, bf16[192,192]{1,0:T(8,128)(2,1)}, u32[]{:S(2)}) copy-start(bf16[192,192]{1,0:T(8,128)(2,1)} %param.8) | copy-start | bytes 221188

commit v2 on v1

--- a/solution.py
+++ b/solution.py
@@ -1,12 +1,20 @@
+import functools
 import math
 
 import jax
 import jax.numpy as jnp
 import numpy as np
 from jax import lax
+from jax.experimental import pallas as pl
+from jax.experimental.pallas import tpu as pltpu
 from jax.sharding import PartitionSpec as P
 
-SPARE = 24
+SPARE = 32
+UNIT = 16
+VMEM_BYTES = 60 * 1024 * 1024
+EARLY = pl.CostEstimate(flops=1, bytes_accessed=1, transcendentals=0)
+LONG = pl.CostEstimate(flops=10**12, bytes_accessed=1, transcendentals=0)
+HALF_CHUNKS = (1, 1, 1, 2, 2, 1, 1, 1)
 
 
 def prolate_basis(width, waves, nlon):
@@ -24,8 +32,19 @@
     return leading * np.where(even, np.where(flat_sign == 0, 1, flat_sign), np.where(lead_sign == 0, 1, lead_sign))
 
 
-def fourier_table(wave_order, nlon):
-    longitude = jnp.arange(nlon, dtype=jnp.int32)
+def factor_tables(width, waves, nlon):
+    exact = prolate_basis(width, waves, nlon)
+    compress = exact.astype(jnp.bfloat16)
+    spread = exact @ np.linalg.inv(compress.astype(np.float64).T @ exact)
+    return compress, spread.astype(np.float32)
+
+
+def fourier_angles(orders, longitude, nlon):
+    phases = orders.reshape(2, -1, 1) * longitude % nlon
+    return phases.astype(jnp.float32) * (2.0 * math.pi / nlon)
+
+
+def fourier_table(wave_order, longitude, nlon):
     phases = wave_order[:, None] * longitude[None, :] % nlon
     angles = phases.astype(jnp.float32) * (2.0 * math.pi / nlon)
     return jnp.stack([jnp.cos(angles), -jnp.sin(angles)]).astype(jnp.bfloat16)
@@ -38,6 +57,417 @@
     return jnp.dot(
         rows.astype(jnp.bfloat16), lons.astype(jnp.bfloat16), preferred_element_type=jnp.float32
     )
+
+
+def params():
+    return pltpu.CompilerParams(vmem_limit_bytes=VMEM_BYTES)
+
+
+def later(arrays):
+    return [pl.BlockSpec(memory_space=pl.ANY)] * len(arrays)
+
+
+def heat_body(core_ref, state_ref, mask_ref, coupling_ref, compress_ref, *rest):
+    out_ref, wide, heated = rest[-3:]
+    levels = state_ref.shape[0]
+    wide[...] = state_ref[...].astype(jnp.float32)
+    for row in range(UNIT):
+        strip = wide[:, row, :]
+        blended = jnp.dot(
+            coupling_ref[...], strip.astype(jnp.bfloat16), preferred_element_type=jnp.float32
+        )
+        heating = (2.0 * jnp.tanh(blended)).astype(jnp.bfloat16).astype(jnp.float32)
+        total = strip + heating * mask_ref[row : row + 1, :]
+        heated[row * levels : (row + 1) * levels, :] = total.astype(jnp.bfloat16)
+    out_ref[0] = lax.dot_general(
+        compress_ref[...],
+        heated[...],
+        (((1,), (1,)), ((), ())),
+        preferred_element_type=jnp.float32,
+    ).astype(jnp.bfloat16)
+
+
+def heat_and_compress(core, state, mask, coupling, compress, first, units, after):
+    levels, band_rows, lon_width = state.shape
+    half_units = band_rows // (2 * UNIT)
+    rank = compress.shape[0]
+
+    def source(side, step, core):
+        half = jnp.where(side == 0, core[0], 1 - core[0])
+        return half * half_units + first + step
+
+    block = UNIT * levels
+    return pl.pallas_call(
+        heat_body,
+        grid_spec=pltpu.PrefetchScalarGridSpec(
+            num_scalar_prefetch=1,
+            grid=(2, units),
+            in_specs=[
+                pl.BlockSpec((levels, UNIT, lon_width), lambda a, b, c: (0, source(a, b, c), 0)),
+                pl.BlockSpec((UNIT, lon_width), lambda a, b, c: (source(a, b, c), 0)),
+                pl.BlockSpec((levels, levels), lambda a, b, c: (0, 0)),
+                pl.BlockSpec((rank, lon_width), lambda a, b, c: (0, 0)),
+            ]
+            + later(after),
+            out_specs=pl.BlockSpec((1, rank, block), lambda a, b, c: (a, 0, b)),
+            scratch_shapes=[
+                pltpu.VMEM((levels, UNIT, lon_width), jnp.float32),
+                pltpu.VMEM((block, lon_width), jnp.bfloat16),
+            ],
+        ),
+        out_shape=jax.ShapeDtypeStruct((2, rank, units * block), jnp.bfloat16),
+        compiler_params=params(),
+        cost_estimate=EARLY,
+    )(core, state, mask, coupling, compress, *after)
+
+
+def join_body(core_ref, mine_ref, arrived_ref, *rest):
+    out_ref = rest[-1]
+    out_ref[0] = jnp.where(core_ref[0] == pl.program_id(0), mine_ref[0], arrived_ref[...])
+
+
+def join_cores(core, both, arrived, after):
+    _, rank, lanes = both.shape
+    return pl.pallas_call(
+        join_body,
+        grid_spec=pltpu.PrefetchScalarGridSpec(
+            num_scalar_prefetch=1,
+            grid=(2,),
+            in_specs=[
+                pl.BlockSpec((1, rank, lanes), lambda a, c: (0, 0, 0)),
+                pl.BlockSpec((rank, lanes), lambda a, c: (0, 0)),
+            ]
+            + later(after),
+            out_specs=pl.BlockSpec((1, rank, lanes), lambda a, c: (a, 0, 0)),
+        ),
+        out_shape=jax.ShapeDtypeStruct(both.shape, jnp.bfloat16),
+        compiler_params=params(),
+        cost_estimate=EARLY,
+    )(core, both, arrived, *after)
+
+
+def choose_body(inner_ref, near_ref, away_ref, *rest):
+    out_ref = rest[-1]
+    out_ref[...] = jnp.where(inner_ref[0] == 1, near_ref[...], away_ref[...])
+
+
+def choose(inner, near, away, after):
+    slots, rows, columns = near.shape
+    step = slots // 4
+    spec = pl.BlockSpec((step, rows, columns), lambda k, c: (k, 0, 0))
+    return pl.pallas_call(
+        choose_body,
+        grid_spec=pltpu.PrefetchScalarGridSpec(
+            num_scalar_prefetch=1,
+            grid=(4,),
+            in_specs=[spec, spec] + later(after),
+            out_specs=spec,
+        ),
+        out_shape=jax.ShapeDtypeStruct(near.shape, jnp.bfloat16),
+        compiler_params=params(),
+        cost_estimate=EARLY,
+    )(inner, near, away, *after)
+
+
+def stack_pieces(a_ref, b_ref):
+    rank, lanes = a_ref.shape[1:]
+    return jnp.concatenate(
+        [a_ref[...].reshape(2 * rank, lanes), b_ref[...].reshape(2 * rank, lanes)], axis=0
+    )
+
+
+def partial_body(expand_ref, a_ref, b_ref, *rest):
+    out_ref = rest[-1]
+    rows = stack_pieces(a_ref, b_ref)
+    for part in range(expand_ref.shape[0]):
+        out_ref[part] = jnp.dot(expand_ref[part], rows, preferred_element_type=jnp.float32).astype(
+            jnp.bfloat16
+        )
+
+
+def partial_sums(expand, pieces, block, after):
+    _, rank, lanes = pieces[0].shape
+    parts, waves, _ = expand.shape
+    return pl.pallas_call(
+        partial_body,
+        grid=(lanes // block,),
+        in_specs=[pl.BlockSpec(expand.shape, lambda i: (0, 0, 0))]
+        + [pl.BlockSpec((2, rank, block), lambda i: (0, 0, i))] * 2
+        + later(after),
+        out_specs=pl.BlockSpec((parts, waves, block), lambda i: (0, 0, i)),
+        out_shape=jax.ShapeDtypeStruct((parts, waves, lanes), jnp.bfloat16),
+        compiler_params=params(),
+        cost_estimate=EARLY,
+    )(expand, *pieces, *after)
+
+
+def total_body(levels, expand_ref, a_ref, b_ref, far_ref, *rest):
+    parts = expand_ref.shape[0]
+    outs, total, laid = rest[-2 - parts : -2], rest[-2], rest[-1]
+    rows = stack_pieces(a_ref, b_ref)
+    slots = total.shape[0] // 2
+    for part, out in enumerate(outs):
+        total[...] = jnp.dot(
+            expand_ref[part], rows, preferred_element_type=jnp.float32
+        ) + far_ref[part].astype(jnp.float32)
+        for row in range(UNIT):
+            lanes = slice(row * levels, (row + 1) * levels)
+            laid[:, row, :] = jnp.concatenate([total[:slots, lanes], total[slots:, lanes]], axis=1)
+        out[...] = laid[...].astype(jnp.bfloat16)
+
+
+def total_sums(expand, pieces, far, levels, after, weight):
+    _, rank, lanes = pieces[0].shape
+    parts, waves, _ = expand.shape
+    block = UNIT * levels
+    slots = waves // 2
+    units = lanes // block
+    shape = jax.ShapeDtypeStruct((slots, units * UNIT, 2 * levels), jnp.bfloat16)
+    return pl.pallas_call(
+        functools.partial(total_body, levels),
+        grid=(units,),
+        in_specs=[pl.BlockSpec(expand.shape, lambda i: (0, 0, 0))]
+        + [pl.BlockSpec((2, rank, block), lambda i: (0, 0, i))] * 2
+        + [pl.BlockSpec((parts, waves, block), lambda i: (0, 0, i))]
+        + later(after),
+        out_specs=[pl.BlockSpec((slots, UNIT, 2 * levels), lambda i: (0, i, 0))] * parts,
+        out_shape=[shape] * parts,
+        scratch_shapes=[
+            pltpu.VMEM((waves, block), jnp.float32),
+            pltpu.VMEM((slots, UNIT, 2 * levels), jnp.float32),
+        ],
+        compiler_params=params(),
+        cost_estimate=weight,
+    )(expand, *pieces, far, *after)
+
+
+def gather_rows(parts, starts, half_rows, column):
+    for part, start in zip(parts, starts):
+        rows = part.shape[3]
+        for side in range(part.shape[0] * 2):
+            first = side * half_rows + start
+            column[first : first + rows, :] = part[side // 2, side % 2, 0]
+
+
+def legendre_body(starts, half_rows, stop, legendre_ref, *rest):
+    parts, out_ref, column, table = rest[: len(starts)], rest[-3], rest[-2], rest[-1]
+    gather_rows(parts, starts, stop, column)
+    for side in range(column.shape[0] // stop):
+        table[side * stop : (side + 1) * stop] = legendre_ref[0, side * half_rows : side * half_rows + stop]
+    out_ref[0] = lax.dot_general(
+        column[...], table[...], (((0,), (0,)), ((), ())), preferred_element_type=jnp.float32
+    )
+
+
+def slot_blocks(parts):
+    return [
+        pl.BlockSpec((part.shape[0], 2, 1) + part.shape[3:], lambda k, *_: (0, 0, k, 0, 0)) for part in parts
+    ]
+
+
+def legendre_start(legendre, parts, starts, half_rows, after):
+    owned_count, nlat, degrees = legendre.shape
+    columns = parts[0].shape[-1]
+    stop = starts[-1] + parts[-1].shape[3]
+    kept = nlat // half_rows * stop
+    return pl.pallas_call(
+        functools.partial(legendre_body, starts, half_rows, stop),
+        grid=(owned_count,),
+        in_specs=[pl.BlockSpec((1, nlat, degrees), lambda k: (k, 0, 0))] + slot_blocks(parts) + later(after),
+        out_specs=pl.BlockSpec((1, columns, degrees), lambda k: (k, 0, 0)),
+        scratch_shapes=[pltpu.VMEM((kept, columns), jnp.bfloat16), pltpu.VMEM((kept, degrees), jnp.bfloat16)],
+        out_shape=jax.ShapeDtypeStruct((owned_count, columns, degrees), jnp.float32),
+        compiler_params=params(),
+        cost_estimate=EARLY,
+    )(legendre, *parts, *after)
+
+
+def legendre_rest_body(starts, mine_ref, legendre_ref, so_far_ref, *rest):
+    parts, out_ref, column, table = rest[: len(starts)], rest[-3], rest[-2], rest[-1]
+    rows = legendre_ref.shape[2]
+    gather_rows(parts, starts, rows, column)
+    for side in range(legendre_ref.shape[1]):
+        table[side * rows : (side + 1) * rows] = legendre_ref[0, side]
+    spectrum = so_far_ref[0] + lax.dot_general(
+        column[...], table[...], (((0,), (0,)), ((), ())), preferred_element_type=jnp.float32
+    )
+    degrees = lax.broadcasted_iota(jnp.int32, spectrum.shape, 1)
+    wave = mine_ref[pl.program_id(0)]
+    out_ref[0] = jnp.where(degrees >= wave, spectrum, 0.0).astype(jnp.bfloat16)
+
+
+def legendre_rest(mine, legendre, parts, starts, half_rows, so_far):
+    owned_count, nlat, degrees = legendre.shape
+    columns = parts[0].shape[-1]
+    rows = half_rows - starts[0]
+    sides = nlat // half_rows
+    starts = [start - starts[0] for start in starts]
+    return pl.pallas_call(
+        functools.partial(legendre_rest_body, starts),
+        grid_spec=pltpu.PrefetchScalarGridSpec(
+            num_scalar_prefetch=1,
+            grid=(owned_count,),
+            in_specs=[
+                pl.BlockSpec((1, sides, rows, degrees), lambda k, m: (k, 0, half_rows // rows - 1, 0)),
+                pl.BlockSpec((1, columns, degrees), lambda k, m: (k, 0, 0)),
+            ]
+            + slot_blocks(parts),
+            out_specs=pl.BlockSpec((1, columns, degrees), lambda k, m: (k, 0, 0)),
+            scratch_shapes=[
+                pltpu.VMEM((sides * rows, columns), jnp.bfloat16),
+                pltpu.VMEM((sides * rows, degrees), jnp.bfloat16),
+            ],
+        ),
+        out_shape=jax.ShapeDtypeStruct((owned_count, columns, degrees), jnp.bfloat16),
+        compiler_params=params(),
+        cost_estimate=EARLY,
+    )(mine, legendre.reshape(owned_count, sides, half_rows, degrees), so_far, *parts)
+
+
+def on_line(grid_state, radiation, cloud_slots, wave_order, legendre):
+    levels, band_rows, lon_width = grid_state.shape
+    groups = lax.axis_size("grid")
+    bands = lax.axis_size("lat")
+    waves = wave_order.shape[0]
+    nlon = lon_width * groups
+    half_rows = band_rows // 2
+    owned_count = legendre.shape[0]
+    here = lax.axis_index("grid")
+    core, chip = here % 2, here // 2
+    side = chip // 2
+    is_inner = (chip == 1) | (chip == 2)
+    inner_chip = jnp.where(side == 0, 1, 2)
+    outer_chip = jnp.where(side == 0, 0, 3)
+
+    compress, spread = factor_tables(lon_width, waves, nlon)
+    rank = compress.shape[1]
+    compress = jnp.asarray(np.ascontiguousarray(compress.T))
+    mask = cloud_mask(cloud_slots, band_rows, lon_width)
+    coupling = radiation.T
+    core_ref = core.astype(jnp.int32).reshape(1)
+    inner_ref = is_inner.astype(jnp.int32).reshape(1)
+
+    chips = jnp.stack([inner_chip, outer_chip])
+    sources = (2 * chips[:, None] + jnp.arange(2, dtype=jnp.int32)).reshape(-1)
+
+    def slots_of(chips):
+        device = (
+            jnp.arange(bands, dtype=jnp.int32)[None, :, None] * groups
+            + 2 * chips[:, None, None]
+            + jnp.arange(2, dtype=jnp.int32)
+        )
+        slot = device[..., None] * owned_count + jnp.arange(owned_count, dtype=jnp.int32)
+        return slot.reshape(-1)
+
+    def expand_for(slots):
+        order = wave_order[slots]
+        near = fourier_angles(order, jnp.arange(lon_width, dtype=jnp.int32), nlon)[:, :, None, :]
+        turn = fourier_angles(order, sources * lon_width, nlon)[:, :, :, None]
+        basis = jnp.stack(
+            [
+                jnp.cos(near) * jnp.cos(turn) - jnp.sin(near) * jnp.sin(turn),
+                -(jnp.sin(near) * jnp.cos(turn) + jnp.cos(near) * jnp.sin(turn)),
+            ],
+            axis=1,
+        ).astype(jnp.bfloat16)
+        table = jnp.einsum(
+            "prkgl,ln->prkgn",
+            basis.astype(jnp.float32),
+            jnp.asarray(spread),
+            precision=lax.Precision.HIGHEST,
+        )
+        table = (table * (1.0 / math.sqrt(nlon))).astype(jnp.bfloat16)
+        return table.reshape(2, slots.shape[0], 4 * rank)
+
+    expand_far = expand_for(slots_of(3 - chips))
+    expand_near = expand_for(slots_of(chips))
+
+    to_inner = [(0, 2), (1, 3), (6, 4), (7, 5)]
+    across = [(2, 4), (3, 5), (4, 2), (5, 3)]
+    to_outer = [(2, 0), (3, 1), (4, 6), (5, 7)]
+    beside = [(i, i ^ 1) for i in range(groups)]
+
+    plane = [
+        [band * groups + 2 * here + core for band in range(bands) for core in range(2)]
+        for here in range(groups // 2)
+    ]
+
+    count = len(HALF_CHUNKS)
+    starts = [sum(HALF_CHUNKS[:i]) for i in range(count)]
+    halves, pieces, sums, totals, owned = {}, {}, {}, {}, {}
+    last = [expand_far]
+
+    def heat(i):
+        halves[i] = heat_and_compress(
+            core_ref, grid_state, mask, coupling, compress, starts[i], HALF_CHUNKS[i], last if i else []
+        )
+        if i:
+            last[:] = [halves[i]]
+
+    def join(i):
+        arrived = lax.ppermute(halves[i][1], "grid", beside)
+        joined = join_cores(core_ref, halves[i], arrived, last)
+        pieces[i] = [joined, lax.ppermute(joined, "grid", to_inner)]
+        last[:] = [joined]
+
+    def send(i, part):
+        expand = expand_far if part is None else expand_far[part : part + 1]
+        sums[i, part] = partial_sums(expand, pieces[i], UNIT * levels, last)
+        last[:] = [sums[i, part]]
+
+    def add(i, part):
+        expand = expand_near if part is None else expand_near[part : part + 1]
+        far = lax.ppermute(sums[i, part], "grid", across)
+        found = total_sums(expand, pieces[i], far, levels, last, LONG if i else EARLY)
+        if part is None:
+            totals[i, 0], totals[i, 1] = found
+        else:
+            totals[i, part] = found[0]
+        last[:] = [found[0]]
+
+    def share(i):
+        away = lax.ppermute(totals[i, 1], "grid", to_outer)
+        after = last + ([owned[i - 1]] if 0 < i < final else [])
+        laid = choose(inner_ref, totals[i, 0], away, after)
+        last[:] = [laid]
+        owned[i] = lax.all_to_all(
+            laid, ("lat", "grid"), split_axis=0, concat_axis=0, axis_index_groups=plane, tiled=True
+        ).reshape((bands, 2, owned_count) + laid.shape[1:])
+
+    final = count - 1
+    rows = [UNIT * i for i in starts]
+    heat(0)
+    join(0)
+    heat(1)
+    heat(2)
+    join(1)
+    join(2)
+    send(0, None)
+    heat(3)
+    send(1, None)
+    join(3)
+    for i in range(final):
+        add(i, None)
+        if i + 3 < count and i > 0:
+            join(i + 3)
+        if i + 4 < count:
+            heat(i + 4)
+        if i > 0:
+            share(i - 1)
+        if i + 2 < final:
+            send(i + 2, None)
+        elif i + 2 == final:
+            send(final, 1)
+            send(final, 0)
+    add(final, 1)
+    share(final - 1)
+    add(final, 0)
+    share(final)
+    so_far = legendre_start(legendre, [owned[k] for k in range(final)], rows[:final], half_rows, last)
+
+    position = lax.axis_index("lat") * groups + here
+    taken = lax.dynamic_slice_in_dim(wave_order, position * owned_count, owned_count)
+    return legendre_rest(taken, legendre, [owned[final]], rows[final:], half_rows, so_far)
 
 
 def on_device(grid_state, radiation, cloud_slots, wave_order, legendre):
@@ -50,20 +480,15 @@
     chunks = 5 if own_rows % 5 == 0 else 1
     chunk_rows = own_rows // chunks
 
-    exact = prolate_basis(lon_width, waves, nlon)
-    rank = exact.shape[1]
-    compress = exact.astype(jnp.bfloat16)
-    spread = exact @ np.linalg.inv(compress.astype(np.float64).T @ exact)
-
-    mask = cloud_mask(cloud_slots, band_rows, lon_width).reshape(
-        groups, own_rows, lon_width
-    )
+    compress, spread = factor_tables(lon_width, waves, nlon)
+    rank = compress.shape[1]
+    mask = cloud_mask(cloud_slots, band_rows, lon_width).reshape(groups, own_rows, lon_width)
     state = grid_state.reshape(levels, groups, own_rows, lon_width)
-    basis = fourier_table(wave_order, nlon).reshape(2, waves, groups, lon_width)
+    basis = fourier_table(wave_order, jnp.arange(nlon, dtype=jnp.int32), nlon)
     expand = jnp.einsum(
         "rkgl,ln->krgn",
-        basis.astype(jnp.float32),
-        jnp.asarray(spread, jnp.float32),
+        basis.reshape(2, waves, groups, lon_width).astype(jnp.float32),
+        jnp.asarray(spread),
         precision=lax.Precision.HIGHEST,
     )
     expand = (expand * (1.0 / math.sqrt(nlon))).astype(jnp.bfloat16)
@@ -111,6 +536,13 @@
         P(("lat", "grid"), None, None),
     )
     out_specs = P(("lat", "grid"), None, None)
+
+    def local(grid_state, radiation, cloud_slots, wave_order, legendre):
+        half_units = sum(HALF_CHUNKS)
+        fits = mesh.shape["grid"] == 8 and grid_state.shape[1] == 2 * UNIT * half_units
+        program = on_line if fits else on_device
+        return program(grid_state, radiation, cloud_slots, wave_order, legendre)
+
     return jax.shard_map(
-        on_device, mesh=mesh, in_specs=in_specs, out_specs=out_specs, check_vma=False
-    )
+        local, mesh=mesh, in_specs=in_specs, out_specs=out_specs, check_vma=False
+    )

time: 1160 us -> 1070 us (0.922)
  Pallas kernels: 0 us -> 511 us
  waiting for transfers between devices: 568 us -> 158 us
  starting transfers between devices: 47 us -> 321 us
  local copies, waits for them, and re-layouts: 317 us -> 55.5 us
  matrix products: 170 us -> 9.23 us
  other arithmetic: 42.7 us -> 9.09 us
    all_to_all x10 -> x8, waiting for transfers between devices: 568 us -> 37.7 us  [share(): lax.all_to_all(laid, ('lat', 'grid'), split_axis=0, concat_axis=0, axis_i...]
    pallas_call x0 -> x44, Pallas kernels: none -> 511 us  [the longest x8 220 us: heat_and_compress(): pl.pallas_call(heat_body, grid_spec=pltpu.PrefetchScalarGridSpec(num_scal...]
    ppermute x0 -> x33, starting transfers between devices: none -> 286 us  [the longest x8 249 us: join(): pieces[i] = [joined, lax.ppermute(joined, 'grid', to_inner)]]
    dot_general x12 -> x2, matrix products: 168 us -> 6.2 us  [expand_for(): jnp.einsum('prkgl,ln->prkgn', basis.astype(jnp.float32), jnp.asarray(spre...]
    ppermute x0 -> x33, waiting for transfers between devices: none -> 120 us  [the longest x8 98.9 us: share(): away = lax.ppermute(totals[i, 1], 'grid', to_outer)]
    reshape x11 -> x2, local copies, waits for them, and re-layouts: 87.5 us -> 5.5 us  [expand_for(): return table.reshape(2, slots.shape[0], 4 * rank)]
    unnamed x16 -> x28, local copies, waits for them, and re-layouts: 74.6 us -> 7.23 us
    transpose x6 -> x0, local copies, waits for them, and re-layouts: 58.8 us -> none  [the longest x5 42 us: on_device(): coefs = coefs.reshape(waves, 2, chunk_rows, levels).transpose(0, 2, 1, 3)]
  transfers between devices with their start and end apart: 10 -> 41, of which waited for: 9 -> 9; matrix products, arithmetic and copies ran while one was open for 31% -> 6% of each run, Pallas kernels for 0% -> 41%
where the time goes in v2:
time: 1070 us; the launch traced here: 1060 us
  Pallas kernels  511 us (48%)
  starting transfers between devices  321 us (30%)
  waiting for transfers between devices  158 us (15%)
  local copies, waits for them, and re-layouts  55.5 us (5%)
    ppermute x8, starting transfers between devices, join(): pieces[i] = [joined, lax.ppermute(joined, 'grid', to_inner)]  249 us
    pallas_call x8, Pallas kernels, heat_and_compress(): pl.pallas_call(heat_body, grid_spec=pltpu.PrefetchScalarGridSpec(num_scal...  220 us
    pallas_call x9, Pallas kernels, total_sums(): pl.pallas_call(functools.partial(total_body, levels), grid=(units,), in_s...  99.8 us
    ppermute x8, waiting for transfers between devices, share(): away = lax.ppermute(totals[i, 1], 'grid', to_outer)  98.9 us
    pallas_call x9, Pallas kernels, partial_sums(): pl.pallas_call(partial_body, grid=(lanes // block,), in_specs=[pl.BlockSp...  72.1 us
    all_to_all x8, waiting for transfers between devices, share(): lax.all_to_all(laid, ('lat', 'grid'), split_axis=0, concat_axis=0, axis_i...  37.7 us
    pallas_call x8, Pallas kernels, choose(): pl.pallas_call(choose_body, grid_spec=pltpu.PrefetchScalarGridSpec(num_sc...  36.3 us
    all_to_all x8, starting transfers between devices, share(): lax.all_to_all(laid, ('lat', 'grid'), split_axis=0, concat_axis=0, axis_i...  35.3 us
  transfers between devices with their start and end apart: 41, of which 9 were waited for; matrix products, arithmetic and copies ran while one was open for 6% of the time, Pallas kernels for 41%

profile of v2, /device:TPU:0, one launch (start us, length us, event | category | flops | bytes accessed | tf_op | source)
XLA Modules:
  0.0 1064.3 jit_solution(7287111594228672218)
XLA Ops:
  5.4 22.7 %shard_map.73.mine_ref = bf16[2,192,3072]{2,1,0:T(8,128)(2,1)} custom-call(s32[1]{0:T(128)} %bitcast.6.core_ref, bf16[192,320,512]{2,1,0:T(8,128)(2,1)} %state_ref.15, f32[320,512]{1,0:T(8,128)} %fusion.mask_ref, bf16[192,192]{1,0:T(8,128)(2,1)} %bitcast.38, bf16[192,512]{1,0:T(8,128)(2,1)} %constant.123.clone.compress_ref), custom_call_target="tpu_custom_call" | custom-call | flops 1 | bytes 1 | tf_op jit(solution)/shard_map/pallas_call | solution.py:100
  48.1 22.5 %shard_map.75.rest_0_.mine_ref = bf16[2,192,3072]{2,1,0:T(8,128)(2,1)} custom-call(s32[1]{0:T(128)} %bitcast.6.core_ref, bf16[192,320,512]{2,1,0:T(8,128)(2,1)} %state_ref.15, f32[320,512]{1,0:T(8,128)} %fusion.mask_ref, bf16[192,192]{1,0:T(8,128)(2,1)} %bitcast.39, bf16[192,512]{1,0:T(8,128)(2,1)} %constant.123.clone.compress_ref, ...), custom_call_target="tpu_custom_call" | custom-call | flops 1 | bytes 1 | tf_op jit(solution)/shard_map/pallas_call | solution.py:100
  72.7 6.0 collective-permute-start.1
  78.7 22.6 %shard_map.76.rest_0_.mine_ref = bf16[2,192,3072]{2,1,0:T(8,128)(2,1)} custom-call(s32[1]{0:T(128)} %bitcast.6.core_ref, bf16[192,320,512]{2,1,0:T(8,128)(2,1)} %state_ref.15, f32[320,512]{1,0:T(8,128)} %fusion.mask_ref, bf16[192,192]{1,0:T(8,128)(2,1)} %bitcast.40, bf16[192,512]{1,0:T(8,128)(2,1)} %constant.123.clone.compress_ref, ...), custom_call_target="tpu_custom_call" | custom-call | flops 1 | bytes 1 | tf_op jit(solution)/shard_map/pallas_call | solution.py:100
  115.7 13.1 %collective-permute-done.1.b_ref = bf16[2,192,3072]{2,1,0:T(8,128)(2,1)} collective-permute-done((bf16[2,192,3072]{2,1,0:T(8,128)(2,1)S(1)}, bf16[2,192,3072]{2,1,0:T(8,128)(2,1)}, u32[]{:S(2)}, u32[]{:S(2)}) %collective-permute-start.1) | collective-permute-done | bytes 2359328 | tf_op jit(solution)/shard_map/ppermute | solution.py:410
  128.8 7.8 shard_map.79.rest_0_
  139.1 42.4 %shard_map.80.rest_0_.mine_ref = bf16[2,192,6144]{2,1,0:T(8,128)(2,1)} custom-call(s32[1]{0:T(128)} %bitcast.6.core_ref, bf16[192,320,512]{2,1,0:T(8,128)(2,1)} %state_ref.15, f32[320,512]{1,0:T(8,128)} %fusion.mask_ref, bf16[192,192]{1,0:T(8,128)(2,1)} %bitcast.41, bf16[192,512]{1,0:T(8,128)(2,1)} %constant.123.clone.compress_ref, ...), custom_call_target="tpu_custom_call" | custom-call | flops 1 | bytes 1 | tf_op jit(solution)/shard_map/pallas_call | solution.py:100
  181.5 7.7 shard_map.81.rest_0_
  198.2 6.6 collective-permute-start.10
  207.1 4.0 multiply_convert_fusion.1
  231.0 4.8 shard_map.82.rest_0_.a_ref
  235.8 3.7 collective-permute-start.14
  239.5 10.2 shard_map.83
  249.7 42.0 %shard_map.84.rest_0_.mine_ref = bf16[2,192,6144]{2,1,0:T(8,128)(2,1)} custom-call(s32[1]{0:T(128)} %bitcast.6.core_ref, bf16[192,320,512]{2,1,0:T(8,128)(2,1)} %state_ref.15, f32[320,512]{1,0:T(8,128)} %fusion.mask_ref, bf16[192,192]{1,0:T(8,128)(2,1)} %bitcast.42, bf16[192,512]{1,0:T(8,128)(2,1)} %constant.123.clone.compress_ref, ...), custom_call_target="tpu_custom_call" | custom-call | flops 1 | bytes 1 | tf_op jit(solution)/shard_map/pallas_call | solution.py:100
  296.9 7.9 shard_map.85.rest_0_
  307.4 10.1 shard_map.86
  317.5 4.7 shard_map.87.rest_0_.a_ref
  323.7 22.5 %shard_map.88.rest_0_.mine_ref = bf16[2,192,3072]{2,1,0:T(8,128)(2,1)} custom-call(s32[1]{0:T(128)} %bitcast.6.core_ref, bf16[192,320,512]{2,1,0:T(8,128)(2,1)} %state_ref.15, f32[320,512]{1,0:T(8,128)} %fusion.mask_ref, bf16[192,192]{1,0:T(8,128)(2,1)} %bitcast.43, bf16[192,512]{1,0:T(8,128)(2,1)} %constant.123.clone.compress_ref, ...), custom_call_target="tpu_custom_call" | custom-call | flops 1 | bytes 1 | tf_op jit(solution)/shard_map/pallas_call | solution.py:100
  346.2 10.1 collective-permute-start.18
  358.6 4.2 shard_map.89.rest_0_
  362.9 4.5 all-to-all-start
  367.4 11.0 %shard_map.90.rest_0_ = bf16[2,320,6144]{2,1,0:T(8,128)(2,1)} custom-call(bf16[2,320,768]{2,1,0:T(8,128)(2,1)} %reshape.437.rest_0_.expand_ref, bf16[2,192,6144]{2,1,0:T(8,128)(2,1)} %shard_map.82.rest_0_.a_ref, bf16[2,192,6144]{2,1,0:T(8,128)(2,1)} %collective-permute-done.14.b_ref, bf16[160,16,384]{2,1,0:T(8,128)(2,1)} %shard_map.89.rest_0_), custom_call_target="tpu_custom_call" | custom-call | flops 1 | bytes 1 | tf_op jit(solution)/shard_map/pallas_call | solution.py:191
  378.5 3.8 collective-permute-start.17
  382.2 10.1 shard_map.91
  397.2 22.4 %shard_map.93.rest_0_.mine_ref = bf16[2,192,3072]{2,1,0:T(8,128)(2,1)} custom-call(s32[1]{0:T(128)} %bitcast.6.core_ref, bf16[192,320,512]{2,1,0:T(8,128)(2,1)} %state_ref.15, f32[320,512]{1,0:T(8,128)} %fusion.mask_ref, bf16[192,192]{1,0:T(8,128)(2,1)} %bitcast.44, bf16[192,512]{1,0:T(8,128)(2,1)} %constant.123.clone.compress_ref, ...), custom_call_target="tpu_custom_call" | custom-call | flops 1 | bytes 1 | tf_op jit(solution)/shard_map/pallas_call | solution.py:100
  419.6 19.8 %collective-permute-start.22 = (bf16[2,192,3072]{2,1,0:T(8,128)(2,1)}, bf16[2,192,3072]{2,1,0:T(8,128)(2,1)}, u32[]{:S(2)}, u32[]{:S(2)}) collective-permute-start(bf16[2,192,3072]{2,1,0:T(8,128)(2,1)} %shard_map.92.rest_0_.a_ref), channel_id=1, source_target_pairs={{0,2},{1,3},{6,4},{7,5},{8,10},{9,11},{14,12},{15,13},{16,18},{17,... | collective-permute-start | bytes 7077896 | tf_op jit(solution)/shard_map/ppermute | solution.py:410
  443.1 4.2 shard_map.94.rest_0_
  447.2 4.8 all-to-all-start.1
  452.0 5.3 collective-permute-done.18.b_ref
  457.3 11.0 %shard_map.95.rest_0_ = bf16[2,320,6144]{2,1,0:T(8,128)(2,1)} custom-call(bf16[2,320,768]{2,1,0:T(8,128)(2,1)} %reshape.437.rest_0_.expand_ref, bf16[2,192,6144]{2,1,0:T(8,128)(2,1)} %shard_map.87.rest_0_.a_ref, bf16[2,192,6144]{2,1,0:T(8,128)(2,1)} %collective-permute-done.18.b_ref, bf16[160,16,384]{2,1,0:T(8,128)(2,1)} %shard_map.94.rest_0_), custom_call_target="tpu_custom_call" | custom-call | flops 1 | bytes 1 | tf_op jit(solution)/shard_map/pallas_call | solution.py:191
  468.3 3.8 collective-permute-start.21
  472.1 17.3 %shard_map.96 = (bf16[160,32,384]{2,1,0:T(8,128)(2,1)}, bf16[160,32,384]{2,1,0:T(8,128)(2,1)}) custom-call(bf16[2,320,768]{2,1,0:T(8,128)(2,1)} %reshape.434.expand_ref, bf16[2,192,6144]{2,1,0:T(8,128)(2,1)} %shard_map.82.rest_0_.a_ref, bf16[2,192,6144]{2,1,0:T(8,128)(2,1)} %collective-permute-done.14.b_ref, ...), custom_call_target="tpu_custom_call" | custom-call | flops 999999995904 | bytes 1 | tf_op jit(solution)/shard_map/pallas_call | solution.py:226
  494.1 22.5 %shard_map.98.rest_0_.mine_ref = bf16[2,192,3072]{2,1,0:T(8,128)(2,1)} custom-call(s32[1]{0:T(128)} %bitcast.6.core_ref, bf16[192,320,512]{2,1,0:T(8,128)(2,1)} %state_ref.15, f32[320,512]{1,0:T(8,128)} %fusion.mask_ref, bf16[192,192]{1,0:T(8,128)(2,1)} %bitcast.45, bf16[192,512]{1,0:T(8,128)(2,1)} %constant.123.clone.compress_ref, ...), custom_call_target="tpu_custom_call" | custom-call | flops 1 | bytes 1 | tf_op jit(solution)/shard_map/pallas_call | solution.py:100
  516.6 98.6 %collective-permute-start.25 = (bf16[2,192,3072]{2,1,0:T(8,128)(2,1)}, bf16[2,192,3072]{2,1,0:T(8,128)(2,1)}, u32[]{:S(2)}, u32[]{:S(2)}) collective-permute-start(bf16[2,192,3072]{2,1,0:T(8,128)(2,1)} %shard_map.97.rest_0_.a_ref), channel_id=1, source_target_pairs={{0,2},{1,3},{6,4},{7,5},{8,10},{9,11},{14,12},{15,13},{16,18},{17,... | collective-permute-start | bytes 7077896 | tf_op jit(solution)/shard_map/ppermute | solution.py:410
  617.6 4.2 shard_map.99.rest_0_
  621.8 4.3 all-to-all-start.2
  627.6 7.8 shard_map.100.rest_0_
  638.0 17.5 %shard_map.101 = (bf16[160,32,384]{2,1,0:T(8,128)(2,1)}, bf16[160,32,384]{2,1,0:T(8,128)(2,1)}) custom-call(bf16[2,320,768]{2,1,0:T(8,128)(2,1)} %reshape.434.expand_ref, bf16[2,192,6144]{2,1,0:T(8,128)(2,1)} %shard_map.87.rest_0_.a_ref, bf16[2,192,6144]{2,1,0:T(8,128)(2,1)} %collective-permute-done.18.b_ref, ...), custom_call_target="tpu_custom_call" | custom-call | flops 999999995904 | bytes 1 | tf_op jit(solution)/shard_map/pallas_call | solution.py:226
  658.7 101.2 %collective-permute-start.28 = (bf16[2,192,3072]{2,1,0:T(8,128)(2,1)}, bf16[2,192,3072]{2,1,0:T(8,128)(2,1)}, u32[]{:S(2)}, u32[]{:S(2)}) collective-permute-start(bf16[2,192,3072]{2,1,0:T(8,128)(2,1)} %shard_map.102.rest_0_.a_ref), channel_id=1, source_target_pairs={{0,2},{1,3},{6,4},{7,5},{8,10},{9,11},{14,12},{15,13},{16,18},{17,... | collective-permute-start | bytes 7077896 | tf_op jit(solution)/shard_map/ppermute | solution.py:410
  759.9 5.6 shard_map.103.rest_0_
  765.5 4.5 all-to-all-start.3
  771.3 7.8 shard_map.104.rest_0_
  782.1 10.2 shard_map.105
  793.6 22.8 %all-to-all-done.3 = bf16[160,32,384]{2,1,0:T(8,128)(2,1)} async-done(((bf16[160,32,384]{2,1,0:T(8,128)(2,1)}), bf16[160,32,384]{2,1,0:T(8,128)(2,1)}, u32[]{:S(2)}, u32[]{:S(2)}) %all-to-all-start.3) | async-done | bytes 3932192 | tf_op jit(solution)/shard_map/all_to_all | solution.py:433
  816.3 43.7 %collective-permute-done.23.away_ref = bf16[160,32,384]{2,1,0:T(8,128)(2,1)} collective-permute-done((bf16[160,32,384]{2,1,0:T(8,128)(2,1)}, bf16[160,32,384]{2,1,0:T(8,128)(2,1)}, u32[]{:S(2)}, u32[]{:S(2)}) %collective-permute-start.23) | collective-permute-done | bytes 3932192 | tf_op jit(solution)/shard_map/ppermute | solution.py:429
  860.0 5.6 shard_map.106.rest_0_
  865.6 4.5 all-to-all-start.4
  870.2 5.5 shard_map.107.rest_0_
  877.7 5.5 shard_map.108.rest_0_
  885.1 10.2 shard_map.109
  896.6 5.0 collective-permute-done.26.away_ref
  901.6 14.9 %all-to-all-done.4 = bf16[160,32,384]{2,1,0:T(8,128)(2,1)} async-done(((bf16[160,32,384]{2,1,0:T(8,128)(2,1)}), bf16[160,32,384]{2,1,0:T(8,128)(2,1)}, u32[]{:S(2)}, u32[]{:S(2)}) %all-to-all-start.4) | async-done | bytes 3932192 | tf_op jit(solution)/shard_map/all_to_all | solution.py:433
  916.5 4.2 shard_map.110.rest_0_
  920.7 4.5 all-to-all-start.5
  925.2 7.1 shard_map.111.rest_0_
  933.6 26.2 %collective-permute-done.29.away_ref = bf16[160,16,384]{2,1,0:T(8,128)(2,1)} collective-permute-done((bf16[160,16,384]{2,1,0:T(8,128)(2,1)}, bf16[160,16,384]{2,1,0:T(8,128)(2,1)}, u32[]{:S(2)}, u32[]{:S(2)}) %collective-permute-start.29) | collective-permute-done | bytes 1966112 | tf_op jit(solution)/shard_map/ppermute | solution.py:429
  959.8 4.1 shard_map.112.rest_0_
  964.0 4.4 all-to-all-start.6
  968.3 7.1 shard_map.113.near_ref.rest_0_
  975.4 24.0 %collective-permute-done.32.away_ref = bf16[160,16,384]{2,1,0:T(8,128)(2,1)} collective-permute-done((bf16[160,16,384]{2,1,0:T(8,128)(2,1)}, bf16[160,16,384]{2,1,0:T(8,128)(2,1)}, u32[]{:S(2)}, u32[]{:S(2)}) %collective-permute-start.32) | collective-permute-done | bytes 1966112 | tf_op jit(solution)/shard_map/ppermute | solution.py:429
  999.4 4.2 shard_map.114.rest_7_
  1003.7 3.7 all-to-all-start.7
  1008.7 32.9 %shard_map.115.so_far_ref = f32[20,384,640]{2,1,0:T(8,128)} custom-call(bf16[20,1280,640]{2,1,0:T(8,128)(2,1)} %legendre_ref.1, bf16[4,2,20,16,384]{4,3,2,1,0:T(8,128)(2,1)} %bitcast.14.rest_1_.rest_0_, bf16[4,2,20,16,384]{4,3,2,1,0:T(8,128)(2,1)} %bitcast.16.rest_1_, bf16[4,2,20,16,384]{4,3,2,1,0:T(8,128)(2,1)} %bitcast.18.rest_1_.rest_2_, ...), custom_call_target="tpu_custom_call" | custom-call | flops 1 | bytes 1 | tf_op jit(solution)/shard_map/pallas_call | solution.py:273
  1042.9 21.2 %shard_map.116 = bf16[20,384,640]{2,1,0:T(8,128)(2,1)} custom-call(s32[20]{0:T(128)} %dynamic_slice.3.mine_ref, bf16[20,8,160,640]{3,2,1,0:T(8,128)(2,1)} %bitcast.37, f32[20,384,640]{2,1,0:T(8,128)} %shard_map.115.so_far_ref, bf16[4,2,20,16,384]{4,3,2,1,0:T(8,128)(2,1)} %bitcast.46), custom_call_target="tpu_custom_call" | custom-call | flops 1 | bytes 1 | tf_op jit(solution)/shard_map/pallas_call | solution.py:305
  (141 shorter events, 124.4 us)
Async XLA Ops:
  28.1 2.4 copy-start
  29.5 15.5 %collective-permute-start = (bf16[192,3072]{1,0:T(8,128)(2,1)S(1)}, bf16[192,3072]{1,0:T(8,128)(2,1)}, u32[]{:S(2)}, u32[]{:S(2)}) collective-permute-start(bf16[192,3072]{1,0:T(8,128)(2,1)S(1)} %slice_bitcast_fusion.7), channel_id=1, source_target_pairs={{0,1},{1,0},{2,3},{3,2},{4,5},{5,4},{6,7},{7,6},{8,9},{9,8},{10,11... | collective-permute-start | bytes 3538952 | tf_op jit(solution)/shard_map/ppermute | solution.py:408
  34.9 3.7 copy-start.9
  35.2 3.4 copy-start.11
  40.9 1.1 copy-start.4
  70.7 2.0 copy-start.1
  72.2 29.1 %collective-permute-start.3 = (bf16[192,3072]{1,0:T(8,128)(2,1)S(1)}, bf16[192,3072]{1,0:T(8,128)(2,1)}, u32[]{:S(2)}, u32[]{:S(2)}) collective-permute-start(bf16[192,3072]{1,0:T(8,128)(2,1)S(1)} %slice_bitcast_fusion.5), channel_id=1, source_target_pairs={{0,1},{1,0},{2,3},{3,2},{4,5},{5,4},{6,7},{7,6},{8,9},{9,8},{10,11... | collective-permute-start | bytes 3538952 | tf_op jit(solution)/shard_map/ppermute | solution.py:408
  72.7 56.1 %collective-permute-start.1 = (bf16[2,192,3072]{2,1,0:T(8,128)(2,1)S(1)}, bf16[2,192,3072]{2,1,0:T(8,128)(2,1)}, u32[]{:S(2)}, u32[]{:S(2)}) collective-permute-start(bf16[2,192,3072]{2,1,0:T(8,128)(2,1)S(1)} %copy-done.1), channel_id=1, source_target_pairs={{0,2},{1,3},{6,4},{7,5},{8,10},{9,11},{14,12},{15,13},{16,18},{17,... | collective-permute-start | bytes 7077896 | tf_op jit(solution)/shard_map/ppermute | solution.py:410
  104.5 77.1 %collective-permute-start.6 = (bf16[2,192,3072]{2,1,0:T(8,128)(2,1)}, bf16[2,192,3072]{2,1,0:T(8,128)(2,1)}, u32[]{:S(2)}, u32[]{:S(2)}) collective-permute-start(bf16[2,192,3072]{2,1,0:T(8,128)(2,1)} %shard_map.77.rest_0_.a_ref), channel_id=1, source_target_pairs={{0,2},{1,3},{6,4},{7,5},{8,10},{9,11},{14,12},{15,13},{16,18},{17,... | collective-permute-start | bytes 7077896 | tf_op jit(solution)/shard_map/ppermute | solution.py:410
  108.6 2.9 collective-permute-start.2
  111.5 1.0 copy-start.8
  136.6 102.9 %collective-permute-start.4 = (bf16[2,320,3072]{2,1,0:T(8,128)(2,1)}, bf16[2,320,3072]{2,1,0:T(8,128)(2,1)}, u32[]{:S(2)}, u32[]{:S(2)}) collective-permute-start(bf16[2,320,3072]{2,1,0:T(8,128)(2,1)} %shard_map.79.rest_0_), channel_id=1, source_target_pairs={{2,4},{3,5},{4,2},{5,3},{10,12},{11,13},{12,10},{13,11},{18,20},{1... | collective-permute-start | bytes 11796488 | tf_op jit(solution)/shard_map/ppermute | solution.py:420
  189.3 6.3 copy-start.10
  189.3 8.9 copy-start.2
  189.3 118.1 %collective-permute-start.9 = (bf16[2,320,3072]{2,1,0:T(8,128)(2,1)}, bf16[2,320,3072]{2,1,0:T(8,128)(2,1)}, u32[]{:S(2)}, u32[]{:S(2)}) collective-permute-start(bf16[2,320,3072]{2,1,0:T(8,128)(2,1)} %shard_map.81.rest_0_), channel_id=1, source_target_pairs={{2,4},{3,5},{4,2},{5,3},{10,12},{11,13},{12,10},{13,11},{18,20},{1... | collective-permute-start | bytes 11796488 | tf_op jit(solution)/shard_map/ppermute | solution.py:420
  195.5 11.6 %copy-start.12 = (f32[512,192,1,1,1]{0,1,4,3,2:T(8,128)S(1)}, f32[512,192,1,1,1]{0,1,4,3,2:T(8,128)}, u32[]{:S(2)}) copy-start(f32[512,192,1,1,1]{0,1,4,3,2:T(8,128)} %constant.127) | copy-start | bytes 1179652
  195.5 35.5 %collective-permute-start.5 = (bf16[192,6144]{1,0:T(8,128)(2,1)}, bf16[192,6144]{1,0:T(8,128)(2,1)}, u32[]{:S(2)}, u32[]{:S(2)}) collective-permute-start(bf16[192,6144]{1,0:T(8,128)(2,1)} %slice_bitcast_fusion.1), channel_id=1, source_target_pairs={{0,1},{1,0},{2,3},{3,2},{4,5},{5,4},{6,7},{7,6},{8,9},{9,8},{10,11... | collective-permute-start | bytes 7077896 | tf_op jit(solution)/shard_map/ppermute | solution.py:408
  198.2 98.7 %collective-permute-start.10 = (bf16[2,192,3072]{2,1,0:T(8,128)(2,1)S(1)}, bf16[2,192,3072]{2,1,0:T(8,128)(2,1)}, u32[]{:S(2)}, u32[]{:S(2)}) collective-permute-start(bf16[2,192,3072]{2,1,0:T(8,128)(2,1)S(1)} %copy-done.2), channel_id=1, source_target_pairs={{0,2},{1,3},{6,4},{7,5},{8,10},{9,11},{14,12},{15,13},{16,18},{17,... | collective-permute-start | bytes 7077896 | tf_op jit(solution)/shard_map/ppermute | solution.py:410
  211.1 1.1 copy-start.5
  235.8 131.6 %collective-permute-start.14 = (bf16[2,192,6144]{2,1,0:T(8,128)(2,1)}, bf16[2,192,6144]{2,1,0:T(8,128)(2,1)}, u32[]{:S(2)}, u32[]{:S(2)}) collective-permute-start(bf16[2,192,6144]{2,1,0:T(8,128)(2,1)} %shard_map.82.rest_0_.a_ref), channel_id=1, source_target_pairs={{0,2},{1,3},{6,4},{7,5},{8,10},{9,11},{14,12},{15,13},{16,18},{17,... | collective-permute-start | bytes 14155784 | tf_op jit(solution)/shard_map/ppermute | solution.py:410
  295.0 22.5 %collective-permute-start.8 = (bf16[192,6144]{1,0:T(8,128)(2,1)}, bf16[192,6144]{1,0:T(8,128)(2,1)}, u32[]{:S(2)}, u32[]{:S(2)}) collective-permute-start(bf16[192,6144]{1,0:T(8,128)(2,1)} %slice_bitcast_fusion), channel_id=1, source_target_pairs={{0,1},{1,0},{2,3},{3,2},{4,5},{5,4},{6,7},{7,6},{8,9},{9,8},{10,11... | collective-permute-start | bytes 7077896 | tf_op jit(solution)/shard_map/ppermute | solution.py:408
  295.2 63.5 %collective-permute-start.7 = (bf16[160,16,384]{2,1,0:T(8,128)(2,1)}, bf16[160,16,384]{2,1,0:T(8,128)(2,1)}, u32[]{:S(2)}, u32[]{:S(2)}) collective-permute-start(bf16[160,16,384]{2,1,0:T(8,128)(2,1)} %get-tuple-element.20), channel_id=1, source_target_pairs={{2,0},{3,1},{4,6},{5,7},{10,8},{11,9},{12,14},{13,15},{18,16},{19,... | collective-permute-start | bytes 5898248 | tf_op jit(solution)/shard_map/ppermute | solution.py:429
  304.8 77.4 %collective-permute-start.13 = (bf16[2,320,3072]{2,1,0:T(8,128)(2,1)}, bf16[2,320,3072]{2,1,0:T(8,128)(2,1)}, u32[]{:S(2)}, u32[]{:S(2)}) collective-permute-start(bf16[2,320,3072]{2,1,0:T(8,128)(2,1)} %shard_map.85.rest_0_), channel_id=1, source_target_pairs={{2,4},{3,5},{4,2},{5,3},{10,12},{11,13},{12,10},{13,11},{18,20},{1... | collective-permute-start | bytes 11796488 | tf_op jit(solution)/shard_map/ppermute | solution.py:420
  322.2 119.6 %collective-permute-start.11 = (bf16[160,16,384]{2,1,0:T(8,128)(2,1)}, bf16[160,16,384]{2,1,0:T(8,128)(2,1)}, u32[]{:S(2)}, u32[]{:S(2)}) collective-permute-start(bf16[160,16,384]{2,1,0:T(8,128)(2,1)} %get-tuple-element.22), channel_id=1, source_target_pairs={{2,0},{3,1},{4,6},{5,7},{10,8},{11,9},{12,14},{13,15},{18,16},{19,... | collective-permute-start | bytes 5898248 | tf_op jit(solution)/shard_map/ppermute | solution.py:429
  346.2 111.1 %collective-permute-start.18 = (bf16[2,192,6144]{2,1,0:T(8,128)(2,1)}, bf16[2,192,6144]{2,1,0:T(8,128)(2,1)}, u32[]{:S(2)}, u32[]{:S(2)}) collective-permute-start(bf16[2,192,6144]{2,1,0:T(8,128)(2,1)} %shard_map.87.rest_0_.a_ref), channel_id=1, source_target_pairs={{0,2},{1,3},{6,4},{7,5},{8,10},{9,11},{14,12},{15,13},{16,18},{17,... | collective-permute-start | bytes 14155784 | tf_op jit(solution)/shard_map/ppermute | solution.py:410
  358.6 33.7 %collective-permute-start.12 = (bf16[192,3072]{1,0:T(8,128)(2,1)}, bf16[192,3072]{1,0:T(8,128)(2,1)}, u32[]{:S(2)}, u32[]{:S(2)}) collective-permute-start(bf16[192,3072]{1,0:T(8,128)(2,1)} %slice_bitcast_fusion.4), channel_id=1, source_target_pairs={{0,1},{1,0},{2,3},{3,2},{4,5},{5,4},{6,7},{7,6},{8,9},{9,8},{10,11... | collective-permute-start | bytes 3538952 | tf_op jit(solution)/shard_map/ppermute | solution.py:408
  362.9 80.2 %all-to-all-start = ((bf16[160,16,384]{2,1,0:T(8,128)(2,1)}), bf16[160,16,384]{2,1,0:T(8,128)(2,1)}, u32[]{:S(2)}, u32[]{:S(2)}) async-start(bf16[160,16,384]{2,1,0:T(8,128)(2,1)} %shard_map.89.rest_0_), calls=%async_computation | async-start | bytes 3932160 | tf_op jit(solution)/shard_map/all_to_all | solution.py:433
  378.5 93.6 %collective-permute-start.17 = (bf16[2,320,6144]{2,1,0:T(8,128)(2,1)}, bf16[2,320,6144]{2,1,0:T(8,128)(2,1)}, u32[]{:S(2)}, u32[]{:S(2)}) collective-permute-start(bf16[2,320,6144]{2,1,0:T(8,128)(2,1)} %shard_map.90.rest_0_), channel_id=1, source_target_pairs={{2,4},{3,5},{4,2},{5,3},{10,12},{11,13},{12,10},{13,11},{18,20},{1... | collective-permute-start | bytes 23592968 | tf_op jit(solution)/shard_map/ppermute | solution.py:420
  392.4 3.4 copy-start.6
  419.6 208.0 %collective-permute-start.22 = (bf16[2,192,3072]{2,1,0:T(8,128)(2,1)}, bf16[2,192,3072]{2,1,0:T(8,128)(2,1)}, u32[]{:S(2)}, u32[]{:S(2)}) collective-permute-start(bf16[2,192,3072]{2,1,0:T(8,128)(2,1)} %shard_map.92.rest_0_.a_ref), channel_id=1, source_target_pairs={{0,2},{1,3},{6,4},{7,5},{8,10},{9,11},{14,12},{15,13},{16,18},{17,... | collective-permute-start | bytes 7077896 | tf_op jit(solution)/shard_map/ppermute | solution.py:410
  441.8 47.6 %collective-permute-start.16 = (bf16[192,3072]{1,0:T(8,128)(2,1)}, bf16[192,3072]{1,0:T(8,128)(2,1)}, u32[]{:S(2)}, u32[]{:S(2)}) collective-permute-start(bf16[192,3072]{1,0:T(8,128)(2,1)} %slice_bitcast_fusion.3), channel_id=1, source_target_pairs={{0,1},{1,0},{2,3},{3,2},{4,5},{5,4},{6,7},{7,6},{8,9},{9,8},{10,11... | collective-permute-start | bytes 3538952 | tf_op jit(solution)/shard_map/ppermute | solution.py:408
  441.8 175.8 %collective-permute-start.15 = (bf16[160,16,384]{2,1,0:T(8,128)(2,1)}, bf16[160,16,384]{2,1,0:T(8,128)(2,1)}, u32[]{:S(2)}, u32[]{:S(2)}) collective-permute-start(bf16[160,16,384]{2,1,0:T(8,128)(2,1)} %get-tuple-element.24), channel_id=1, source_target_pairs={{2,0},{3,1},{4,6},{5,7},{10,8},{11,9},{12,14},{13,15},{18,16},{19,... | collective-permute-start | bytes 5898248 | tf_op jit(solution)/shard_map/ppermute | solution.py:429
  447.2 170.4 %all-to-all-start.1 = ((bf16[160,16,384]{2,1,0:T(8,128)(2,1)}), bf16[160,16,384]{2,1,0:T(8,128)(2,1)}, u32[]{:S(2)}, u32[]{:S(2)}) async-start(bf16[160,16,384]{2,1,0:T(8,128)(2,1)} %shard_map.94.rest_0_), calls=%async_computation.1 | async-start | bytes 3932160 | tf_op jit(solution)/shard_map/all_to_all | solution.py:433
  468.3 169.7 %collective-permute-start.21 = (bf16[2,320,6144]{2,1,0:T(8,128)(2,1)}, bf16[2,320,6144]{2,1,0:T(8,128)(2,1)}, u32[]{:S(2)}, u32[]{:S(2)}) collective-permute-start(bf16[2,320,6144]{2,1,0:T(8,128)(2,1)} %shard_map.95.rest_0_), channel_id=1, source_target_pairs={{2,4},{3,5},{4,2},{5,3},{10,12},{11,13},{12,10},{13,11},{18,20},{1... | collective-permute-start | bytes 23592968 | tf_op jit(solution)/shard_map/ppermute | solution.py:420
  489.4 3.3 copy-start.7
  516.6 254.7 %collective-permute-start.25 = (bf16[2,192,3072]{2,1,0:T(8,128)(2,1)}, bf16[2,192,3072]{2,1,0:T(8,128)(2,1)}, u32[]{:S(2)}, u32[]{:S(2)}) collective-permute-start(bf16[2,192,3072]{2,1,0:T(8,128)(2,1)} %shard_map.97.rest_0_.a_ref), channel_id=1, source_target_pairs={{0,2},{1,3},{6,4},{7,5},{8,10},{9,11},{14,12},{15,13},{16,18},{17,... | collective-permute-start | bytes 7077896 | tf_op jit(solution)/shard_map/ppermute | solution.py:410
  617.6 37.9 %collective-permute-start.20 = (bf16[192,3072]{1,0:T(8,128)(2,1)}, bf16[192,3072]{1,0:T(8,128)(2,1)}, u32[]{:S(2)}, u32[]{:S(2)}) collective-permute-start(bf16[192,3072]{1,0:T(8,128)(2,1)} %slice_bitcast_fusion.2), channel_id=1, source_target_pairs={{0,1},{1,0},{2,3},{3,2},{4,5},{5,4},{6,7},{7,6},{8,9},{9,8},{10,11... | collective-permute-start | bytes 3538952 | tf_op jit(solution)/shard_map/ppermute | solution.py:408
  621.8 138.1 %all-to-all-start.2 = ((bf16[160,16,384]{2,1,0:T(8,128)(2,1)}), bf16[160,16,384]{2,1,0:T(8,128)(2,1)}, u32[]{:S(2)}, u32[]{:S(2)}) async-start(bf16[160,16,384]{2,1,0:T(8,128)(2,1)} %shard_map.99.rest_0_), calls=%async_computation.2 | async-start | bytes 3932160 | tf_op jit(solution)/shard_map/all_to_all | solution.py:433
  626.1 133.7 %collective-permute-start.19 = (bf16[160,32,384]{2,1,0:T(8,128)(2,1)}, bf16[160,32,384]{2,1,0:T(8,128)(2,1)}, u32[]{:S(2)}, u32[]{:S(2)}) collective-permute-start(bf16[160,32,384]{2,1,0:T(8,128)(2,1)} %get-tuple-element.26), channel_id=1, source_target_pairs={{2,0},{3,1},{4,6},{5,7},{10,8},{11,9},{12,14},{13,15},{18,16},{19,... | collective-permute-start | bytes 11796488 | tf_op jit(solution)/shard_map/ppermute | solution.py:429
  635.4 146.7 %collective-permute-start.24 = (bf16[2,320,3072]{2,1,0:T(8,128)(2,1)}, bf16[2,320,3072]{2,1,0:T(8,128)(2,1)}, u32[]{:S(2)}, u32[]{:S(2)}) collective-permute-start(bf16[2,320,3072]{2,1,0:T(8,128)(2,1)} %shard_map.100.rest_0_), channel_id=1, source_target_pairs={{2,4},{3,5},{4,2},{5,3},{10,12},{11,13},{12,10},{13,11},{18,20},{1... | collective-permute-start | bytes 11796488 | tf_op jit(solution)/shard_map/ppermute | solution.py:420
  658.7 211.5 %collective-permute-start.28 = (bf16[2,192,3072]{2,1,0:T(8,128)(2,1)}, bf16[2,192,3072]{2,1,0:T(8,128)(2,1)}, u32[]{:S(2)}, u32[]{:S(2)}) collective-permute-start(bf16[2,192,3072]{2,1,0:T(8,128)(2,1)} %shard_map.102.rest_0_.a_ref), channel_id=1, source_target_pairs={{0,2},{1,3},{6,4},{7,5},{8,10},{9,11},{14,12},{15,13},{16,18},{17,... | collective-permute-start | bytes 7077896 | tf_op jit(solution)/shard_map/ppermute | solution.py:410
  765.5 50.9 %all-to-all-start.3 = ((bf16[160,32,384]{2,1,0:T(8,128)(2,1)}), bf16[160,32,384]{2,1,0:T(8,128)(2,1)}, u32[]{:S(2)}, u32[]{:S(2)}) async-start(bf16[160,32,384]{2,1,0:T(8,128)(2,1)} %shard_map.103.rest_0_), calls=%async_computation.3 | async-start | bytes 7864320 | tf_op jit(solution)/shard_map/all_to_all | solution.py:433
  770.0 90.0 %collective-permute-start.23 = (bf16[160,32,384]{2,1,0:T(8,128)(2,1)}, bf16[160,32,384]{2,1,0:T(8,128)(2,1)}, u32[]{:S(2)}, u32[]{:S(2)}) collective-permute-start(bf16[160,32,384]{2,1,0:T(8,128)(2,1)} %get-tuple-element.28), channel_id=1, source_target_pairs={{2,0},{3,1},{4,6},{5,7},{10,8},{11,9},{12,14},{13,15},{18,16},{19,... | collective-permute-start | bytes 11796488 | tf_op jit(solution)/shard_map/ppermute | solution.py:429
  779.2 106.0 %collective-permute-start.27 = (bf16[2,320,3072]{2,1,0:T(8,128)(2,1)}, bf16[2,320,3072]{2,1,0:T(8,128)(2,1)}, u32[]{:S(2)}, u32[]{:S(2)}) collective-permute-start(bf16[2,320,3072]{2,1,0:T(8,128)(2,1)} %shard_map.104.rest_0_), channel_id=1, source_target_pairs={{2,4},{3,5},{4,2},{5,3},{10,12},{11,13},{12,10},{13,11},{18,20},{1... | collective-permute-start | bytes 11796488 | tf_op jit(solution)/shard_map/ppermute | solution.py:420
  792.3 109.3 %collective-permute-start.26 = (bf16[160,16,384]{2,1,0:T(8,128)(2,1)}, bf16[160,16,384]{2,1,0:T(8,128)(2,1)}, u32[]{:S(2)}, u32[]{:S(2)}) collective-permute-start(bf16[160,16,384]{2,1,0:T(8,128)(2,1)} %get-tuple-element.30), channel_id=1, source_target_pairs={{2,0},{3,1},{4,6},{5,7},{10,8},{11,9},{12,14},{13,15},{18,16},{19,... | collective-permute-start | bytes 5898248 | tf_op jit(solution)/shard_map/ppermute | solution.py:429
  865.6 50.9 %all-to-all-start.4 = ((bf16[160,32,384]{2,1,0:T(8,128)(2,1)}), bf16[160,32,384]{2,1,0:T(8,128)(2,1)}, u32[]{:S(2)}, u32[]{:S(2)}) async-start(bf16[160,32,384]{2,1,0:T(8,128)(2,1)} %shard_map.106.rest_0_), calls=%async_computation.4 | async-start | bytes 7864320 | tf_op jit(solution)/shard_map/all_to_all | solution.py:433
  875.7 49.4 %collective-permute-start.30 = (bf16[1,320,3072]{2,1,0:T(8,128)(2,1)}, bf16[1,320,3072]{2,1,0:T(8,128)(2,1)}, u32[]{:S(2)}, u32[]{:S(2)}) collective-permute-start(bf16[1,320,3072]{2,1,0:T(8,128)(2,1)} %shard_map.107.rest_0_), channel_id=1, source_target_pairs={{2,4},{3,5},{4,2},{5,3},{10,12},{11,13},{12,10},{13,11},{18,20},{1... | collective-permute-start | bytes 5898248 | tf_op jit(solution)/shard_map/ppermute | solution.py:420
  883.2 85.2 %collective-permute-start.31 = (bf16[1,320,3072]{2,1,0:T(8,128)(2,1)}, bf16[1,320,3072]{2,1,0:T(8,128)(2,1)}, u32[]{:S(2)}, u32[]{:S(2)}) collective-permute-start(bf16[1,320,3072]{2,1,0:T(8,128)(2,1)} %shard_map.108.rest_0_), channel_id=1, source_target_pairs={{2,4},{3,5},{4,2},{5,3},{10,12},{11,13},{12,10},{13,11},{18,20},{1... | collective-permute-start | bytes 5898248 | tf_op jit(solution)/shard_map/ppermute | solution.py:420
  895.3 64.5 %collective-permute-start.29 = (bf16[160,16,384]{2,1,0:T(8,128)(2,1)}, bf16[160,16,384]{2,1,0:T(8,128)(2,1)}, u32[]{:S(2)}, u32[]{:S(2)}) collective-permute-start(bf16[160,16,384]{2,1,0:T(8,128)(2,1)} %get-tuple-element.32), channel_id=1, source_target_pairs={{2,0},{3,1},{4,6},{5,7},{10,8},{11,9},{12,14},{13,15},{18,16},{19,... | collective-permute-start | bytes 5898248 | tf_op jit(solution)/shard_map/ppermute | solution.py:429
  920.7 39.2 %all-to-all-start.5 = ((bf16[160,16,384]{2,1,0:T(8,128)(2,1)}), bf16[160,16,384]{2,1,0:T(8,128)(2,1)}, u32[]{:S(2)}, u32[]{:S(2)}) async-start(bf16[160,16,384]{2,1,0:T(8,128)(2,1)} %shard_map.110.rest_0_), calls=%async_computation.5 | async-start | bytes 3932160 | tf_op jit(solution)/shard_map/all_to_all | solution.py:433
  932.3 67.1 %collective-permute-start.32 = (bf16[160,16,384]{2,1,0:T(8,128)(2,1)}, bf16[160,16,384]{2,1,0:T(8,128)(2,1)}, u32[]{:S(2)}, u32[]{:S(2)}) collective-permute-start(bf16[160,16,384]{2,1,0:T(8,128)(2,1)} %shard_map.111.rest_0_), channel_id=1, source_target_pairs={{2,0},{3,1},{4,6},{5,7},{10,8},{11,9},{12,14},{13,15},{18,16},{19,... | collective-permute-start | bytes 5898248 | tf_op jit(solution)/shard_map/ppermute | solution.py:429
  964.0 39.7 %all-to-all-start.6 = ((bf16[160,16,384]{2,1,0:T(8,128)(2,1)}), bf16[160,16,384]{2,1,0:T(8,128)(2,1)}, u32[]{:S(2)}, u32[]{:S(2)}) async-start(bf16[160,16,384]{2,1,0:T(8,128)(2,1)} %shard_map.112.rest_0_), calls=%async_computation.6 | async-start | bytes 3932160 | tf_op jit(solution)/shard_map/all_to_all | solution.py:433
  1003.7 37.9 %all-to-all-start.7 = ((bf16[160,16,384]{2,1,0:T(8,128)(2,1)}), bf16[160,16,384]{2,1,0:T(8,128)(2,1)S(1)}, u32[]{:S(2)}, u32[]{:S(2)}) async-start(bf16[160,16,384]{2,1,0:T(8,128)(2,1)} %shard_map.114.rest_7_), calls=%async_computation.7 | async-start | bytes 3932160 | tf_op jit(solution)/shard_map/all_to_all | solution.py:433
  1041.5 1.3 copy-start.3

commit v3 on v2

--- a/solution.py
+++ b/solution.py
@@ -241,12 +241,12 @@
     )(expand, *pieces, far, *after)
 
 
-def gather_rows(parts, starts, half_rows, column):
+def gather_rows(parts, starts, half_rows, column, slot=0):
     for part, start in zip(parts, starts):
         rows = part.shape[3]
         for side in range(part.shape[0] * 2):
             first = side * half_rows + start
-            column[first : first + rows, :] = part[side // 2, side % 2, 0]
+            column[first : first + rows, :] = part[side // 2, side % 2, slot]
 
 
 def legendre_body(starts, half_rows, stop, legendre_ref, *rest):
@@ -259,9 +259,10 @@
     )
 
 
-def slot_blocks(parts):
+def slot_blocks(parts, group=1):
     return [
-        pl.BlockSpec((part.shape[0], 2, 1) + part.shape[3:], lambda k, *_: (0, 0, k, 0, 0)) for part in parts
+        pl.BlockSpec((part.shape[0], 2, group) + part.shape[3:], lambda k, *_: (0, 0, k, 0, 0))
+        for part in parts
     ]
 
 
@@ -285,15 +286,17 @@
 def legendre_rest_body(starts, mine_ref, legendre_ref, so_far_ref, *rest):
     parts, out_ref, column, table = rest[: len(starts)], rest[-3], rest[-2], rest[-1]
     rows = legendre_ref.shape[2]
-    gather_rows(parts, starts, rows, column)
-    for side in range(legendre_ref.shape[1]):
-        table[side * rows : (side + 1) * rows] = legendre_ref[0, side]
-    spectrum = so_far_ref[0] + lax.dot_general(
-        column[...], table[...], (((0,), (0,)), ((), ())), preferred_element_type=jnp.float32
-    )
-    degrees = lax.broadcasted_iota(jnp.int32, spectrum.shape, 1)
-    wave = mine_ref[pl.program_id(0)]
-    out_ref[0] = jnp.where(degrees >= wave, spectrum, 0.0).astype(jnp.bfloat16)
+    group = out_ref.shape[0]
+    for slot in range(group):
+        gather_rows(parts, starts, rows, column, slot)
+        for side in range(legendre_ref.shape[1]):
+            table[side * rows : (side + 1) * rows] = legendre_ref[slot, side]
+        spectrum = so_far_ref[slot] + lax.dot_general(
+            column[...], table[...], (((0,), (0,)), ((), ())), preferred_element_type=jnp.float32
+        )
+        degrees = lax.broadcasted_iota(jnp.int32, spectrum.shape, 1)
+        wave = mine_ref[pl.program_id(0) * group + slot]
+        out_ref[slot] = jnp.where(degrees >= wave, spectrum, 0.0).astype(jnp.bfloat16)
 
 
 def legendre_rest(mine, legendre, parts, starts, half_rows, so_far):
@@ -302,17 +305,18 @@
     rows = half_rows - starts[0]
     sides = nlat // half_rows
     starts = [start - starts[0] for start in starts]
+    group = 2 if owned_count % 2 == 0 else 1
     return pl.pallas_call(
         functools.partial(legendre_rest_body, starts),
         grid_spec=pltpu.PrefetchScalarGridSpec(
             num_scalar_prefetch=1,
-            grid=(owned_count,),
+            grid=(owned_count // group,),
             in_specs=[
-                pl.BlockSpec((1, sides, rows, degrees), lambda k, m: (k, 0, half_rows // rows - 1, 0)),
-                pl.BlockSpec((1, columns, degrees), lambda k, m: (k, 0, 0)),
+                pl.BlockSpec((group, sides, rows, degrees), lambda k, m: (k, 0, half_rows // rows - 1, 0)),
+                pl.BlockSpec((group, columns, degrees), lambda k, m: (k, 0, 0)),
             ]
-            + slot_blocks(parts),
-            out_specs=pl.BlockSpec((1, columns, degrees), lambda k, m: (k, 0, 0)),
+            + slot_blocks(parts, group),
+            out_specs=pl.BlockSpec((group, columns, degrees), lambda k, m: (k, 0, 0)),
             scratch_shapes=[
                 pltpu.VMEM((sides * rows, columns), jnp.bfloat16),
                 pltpu.VMEM((sides * rows, degrees), jnp.bfloat16),
@@ -440,9 +444,9 @@
     join(0)
     heat(1)
     heat(2)
+    send(0, None)
     join(1)
     join(2)
-    send(0, None)
     heat(3)
     send(1, None)
     join(3)
@@ -450,11 +454,13 @@
         add(i, None)
         if i + 3 < count and i > 0:
             join(i + 3)
+        if i == 0:
+            send(2, None)
         if i + 4 < count:
             heat(i + 4)
         if i > 0:
             share(i - 1)
-        if i + 2 < final:
+        if 0 < i and i + 2 < final:
             send(i + 2, None)
         elif i + 2 == final:
             send(final, 1)

time: 1070 us -> 1050 us (0.981)
  starting transfers between devices: 321 us -> 297 us
  waiting for transfers between devices: 158 us -> 170 us
    ppermute x8, starting transfers between devices: 249 us -> 225 us  [join(): pieces[i] = [joined, lax.ppermute(joined, 'grid', to_inner)]]
    ppermute x8, waiting for transfers between devices: 18.4 us -> 32.6 us  [join(): pieces[i] = [joined, lax.ppermute(joined, 'grid', to_inner)]]
  transfers between devices with their start and end apart: 41 -> 41, of which waited for: 9 -> 10; matrix products, arithmetic and copies ran while one was open for 6% -> 6% of each run, Pallas kernels for 41% -> 44%
where the time goes in v3:
time: 1050 us
  Pallas kernels  507 us (48%)
  starting transfers between devices  297 us (28%)
  waiting for transfers between devices  170 us (16%)
  local copies, waits for them, and re-layouts  57.7 us (5%)
    ppermute x8, starting transfers between devices, join(): pieces[i] = [joined, lax.ppermute(joined, 'grid', to_inner)]  225 us
    pallas_call x8, Pallas kernels, heat_and_compress(): pl.pallas_call(heat_body, grid_spec=pltpu.PrefetchScalarGridSpec(num_scal...  220 us
    pallas_call x9, Pallas kernels, total_sums(): pl.pallas_call(functools.partial(total_body, levels), grid=(units,), in_s...  99.9 us
    ppermute x8, waiting for transfers between devices, share(): away = lax.ppermute(totals[i, 1], 'grid', to_outer)  99.4 us
    pallas_call x9, Pallas kernels, partial_sums(): pl.pallas_call(partial_body, grid=(lanes // block,), in_specs=[pl.BlockSp...  72.4 us
    all_to_all x8, waiting for transfers between devices, share(): lax.all_to_all(laid, ('lat', 'grid'), split_axis=0, concat_axis=0, axis_i...  37.9 us
    pallas_call x8, Pallas kernels, choose(): pl.pallas_call(choose_body, grid_spec=pltpu.PrefetchScalarGridSpec(num_sc...  36.2 us
    all_to_all x8, starting transfers between devices, share(): lax.all_to_all(laid, ('lat', 'grid'), split_axis=0, concat_axis=0, axis_i...  34.7 us
  transfers between devices with their start and end apart: 41, of which 10 were waited for; matrix products, arithmetic and copies ran while one was open for 6% of the time, Pallas kernels for 44%

profile of v3, /device:TPU:0, one launch (start us, length us, event | category | flops | bytes accessed | tf_op | source)
XLA Modules:
  0.0 1047.3 jit_solution(17898718537617364125)
XLA Ops:
  5.4 22.5 %shard_map.73.mine_ref = bf16[2,192,3072]{2,1,0:T(8,128)(2,1)} custom-call(s32[1]{0:T(128)} %bitcast.6.core_ref, bf16[192,320,512]{2,1,0:T(8,128)(2,1)} %state_ref.15, f32[320,512]{1,0:T(8,128)} %fusion.mask_ref, bf16[192,192]{1,0:T(8,128)(2,1)} %bitcast.38, bf16[192,512]{1,0:T(8,128)(2,1)} %constant.123.clone.compress_ref), custom_call_target="tpu_custom_call" | custom-call | flops 1 | bytes 1 | tf_op jit(solution)/shard_map/pallas_call | solution.py:100
  47.7 4.7 collective-permute-start.1
  52.3 22.8 %shard_map.75.rest_0_.mine_ref = bf16[2,192,3072]{2,1,0:T(8,128)(2,1)} custom-call(s32[1]{0:T(128)} %bitcast.6.core_ref, bf16[192,320,512]{2,1,0:T(8,128)(2,1)} %state_ref.15, f32[320,512]{1,0:T(8,128)} %fusion.mask_ref, bf16[192,192]{1,0:T(8,128)(2,1)} %bitcast.39, bf16[192,512]{1,0:T(8,128)(2,1)} %constant.123.clone.compress_ref, ...), custom_call_target="tpu_custom_call" | custom-call | flops 1 | bytes 1 | tf_op jit(solution)/shard_map/pallas_call | solution.py:100
  77.7 22.6 %shard_map.76.rest_0_.mine_ref = bf16[2,192,3072]{2,1,0:T(8,128)(2,1)} custom-call(s32[1]{0:T(128)} %bitcast.6.core_ref, bf16[192,320,512]{2,1,0:T(8,128)(2,1)} %state_ref.15, f32[320,512]{1,0:T(8,128)} %fusion.mask_ref, bf16[192,192]{1,0:T(8,128)(2,1)} %bitcast.40, bf16[192,512]{1,0:T(8,128)(2,1)} %constant.123.clone.compress_ref, ...), custom_call_target="tpu_custom_call" | custom-call | flops 1 | bytes 1 | tf_op jit(solution)/shard_map/pallas_call | solution.py:100
  105.0 7.8 shard_map.77.rest_0_
  117.2 5.7 collective-permute-start.6
  130.1 41.9 %shard_map.80.rest_0_.mine_ref = bf16[2,192,6144]{2,1,0:T(8,128)(2,1)} custom-call(s32[1]{0:T(128)} %bitcast.6.core_ref, bf16[192,320,512]{2,1,0:T(8,128)(2,1)} %state_ref.15, f32[320,512]{1,0:T(8,128)} %fusion.mask_ref, bf16[192,192]{1,0:T(8,128)(2,1)} %bitcast.41, bf16[192,512]{1,0:T(8,128)(2,1)} %constant.123.clone.compress_ref, ...), custom_call_target="tpu_custom_call" | custom-call | flops 1 | bytes 1 | tf_op jit(solution)/shard_map/pallas_call | solution.py:100
  172.1 7.8 shard_map.81.rest_0_
  186.8 6.3 collective-permute-start.8
  201.9 3.7 reshape.434.expand_ref
  218.4 4.9 shard_map.82.rest_0_.a_ref
  223.3 10.1 shard_map.83
  233.4 9.3 collective-permute-done.8.b_ref
  242.7 7.8 shard_map.84.rest_0_
  250.5 6.6 collective-permute-start.14
  257.1 42.3 %shard_map.85.rest_0_.mine_ref = bf16[2,192,6144]{2,1,0:T(8,128)(2,1)} custom-call(s32[1]{0:T(128)} %bitcast.6.core_ref, bf16[192,320,512]{2,1,0:T(8,128)(2,1)} %state_ref.15, f32[320,512]{1,0:T(8,128)} %fusion.mask_ref, bf16[192,192]{1,0:T(8,128)(2,1)} %bitcast.42, bf16[192,512]{1,0:T(8,128)(2,1)} %constant.123.clone.compress_ref, ...), custom_call_target="tpu_custom_call" | custom-call | flops 1 | bytes 1 | tf_op jit(solution)/shard_map/pallas_call | solution.py:100
  306.7 10.2 shard_map.86
  316.9 5.0 shard_map.87.rest_0_.a_ref
  323.2 22.4 %shard_map.88.rest_0_.mine_ref = bf16[2,192,3072]{2,1,0:T(8,128)(2,1)} custom-call(s32[1]{0:T(128)} %bitcast.6.core_ref, bf16[192,320,512]{2,1,0:T(8,128)(2,1)} %state_ref.15, f32[320,512]{1,0:T(8,128)} %fusion.mask_ref, bf16[192,192]{1,0:T(8,128)(2,1)} %bitcast.43, bf16[192,512]{1,0:T(8,128)(2,1)} %constant.123.clone.compress_ref, ...), custom_call_target="tpu_custom_call" | custom-call | flops 1 | bytes 1 | tf_op jit(solution)/shard_map/pallas_call | solution.py:100
  345.7 8.0 collective-permute-start.18
  356.0 4.2 shard_map.89.rest_0_
  360.2 4.3 all-to-all-start
  365.9 11.2 %shard_map.90.rest_0_ = bf16[2,320,6144]{2,1,0:T(8,128)(2,1)} custom-call(bf16[2,320,768]{2,1,0:T(8,128)(2,1)} %reshape.437.rest_0_.expand_ref, bf16[2,192,6144]{2,1,0:T(8,128)(2,1)} %shard_map.82.rest_0_.a_ref, bf16[2,192,6144]{2,1,0:T(8,128)(2,1)} %collective-permute-done.14.b_ref, bf16[160,16,384]{2,1,0:T(8,128)(2,1)} %shard_map.89.rest_0_), custom_call_target="tpu_custom_call" | custom-call | flops 1 | bytes 1 | tf_op jit(solution)/shard_map/pallas_call | solution.py:191
  377.1 3.8 collective-permute-start.17
  380.9 10.1 shard_map.91
  396.0 22.4 %shard_map.93.rest_0_.mine_ref = bf16[2,192,3072]{2,1,0:T(8,128)(2,1)} custom-call(s32[1]{0:T(128)} %bitcast.6.core_ref, bf16[192,320,512]{2,1,0:T(8,128)(2,1)} %state_ref.15, f32[320,512]{1,0:T(8,128)} %fusion.mask_ref, bf16[192,192]{1,0:T(8,128)(2,1)} %bitcast.44, bf16[192,512]{1,0:T(8,128)(2,1)} %constant.123.clone.compress_ref, ...), custom_call_target="tpu_custom_call" | custom-call | flops 1 | bytes 1 | tf_op jit(solution)/shard_map/pallas_call | solution.py:100
  418.4 8.1 collective-permute-start.22
  430.2 4.1 shard_map.94.rest_0_
  434.3 4.5 all-to-all-start.1
  438.9 19.8 %collective-permute-done.18.b_ref = bf16[2,192,6144]{2,1,0:T(8,128)(2,1)} collective-permute-done((bf16[2,192,6144]{2,1,0:T(8,128)(2,1)}, bf16[2,192,6144]{2,1,0:T(8,128)(2,1)}, u32[]{:S(2)}, u32[]{:S(2)}) %collective-permute-start.18) | collective-permute-done | bytes 4718624 | tf_op jit(solution)/shard_map/ppermute | solution.py:414
  458.7 11.0 %shard_map.95.rest_0_ = bf16[2,320,6144]{2,1,0:T(8,128)(2,1)} custom-call(bf16[2,320,768]{2,1,0:T(8,128)(2,1)} %reshape.437.rest_0_.expand_ref, bf16[2,192,6144]{2,1,0:T(8,128)(2,1)} %shard_map.87.rest_0_.a_ref, bf16[2,192,6144]{2,1,0:T(8,128)(2,1)} %collective-permute-done.18.b_ref, bf16[160,16,384]{2,1,0:T(8,128)(2,1)} %shard_map.94.rest_0_), custom_call_target="tpu_custom_call" | custom-call | flops 1 | bytes 1 | tf_op jit(solution)/shard_map/pallas_call | solution.py:191
  469.7 3.8 collective-permute-start.21
  473.5 17.3 %shard_map.96 = (bf16[160,32,384]{2,1,0:T(8,128)(2,1)}, bf16[160,32,384]{2,1,0:T(8,128)(2,1)}) custom-call(bf16[2,320,768]{2,1,0:T(8,128)(2,1)} %reshape.434.expand_ref, bf16[2,192,6144]{2,1,0:T(8,128)(2,1)} %shard_map.82.rest_0_.a_ref, bf16[2,192,6144]{2,1,0:T(8,128)(2,1)} %collective-permute-done.14.b_ref, ...), custom_call_target="tpu_custom_call" | custom-call | flops 999999995904 | bytes 1 | tf_op jit(solution)/shard_map/pallas_call | solution.py:226
  495.5 22.7 %shard_map.98.rest_0_.mine_ref = bf16[2,192,3072]{2,1,0:T(8,128)(2,1)} custom-call(s32[1]{0:T(128)} %bitcast.6.core_ref, bf16[192,320,512]{2,1,0:T(8,128)(2,1)} %state_ref.15, f32[320,512]{1,0:T(8,128)} %fusion.mask_ref, bf16[192,192]{1,0:T(8,128)(2,1)} %bitcast.45, bf16[192,512]{1,0:T(8,128)(2,1)} %constant.123.clone.compress_ref, ...), custom_call_target="tpu_custom_call" | custom-call | flops 1 | bytes 1 | tf_op jit(solution)/shard_map/pallas_call | solution.py:100
  518.1 85.0 %collective-permute-start.25 = (bf16[2,192,3072]{2,1,0:T(8,128)(2,1)}, bf16[2,192,3072]{2,1,0:T(8,128)(2,1)}, u32[]{:S(2)}, u32[]{:S(2)}) collective-permute-start(bf16[2,192,3072]{2,1,0:T(8,128)(2,1)} %shard_map.97.rest_0_.a_ref), channel_id=1, source_target_pairs={{0,2},{1,3},{6,4},{7,5},{8,10},{9,11},{14,12},{15,13},{16,18},{17,... | collective-permute-start | bytes 7077896 | tf_op jit(solution)/shard_map/ppermute | solution.py:414
  605.5 4.2 shard_map.99.rest_0_
  609.7 4.3 all-to-all-start.2
  615.7 7.9 shard_map.100.rest_0_
  626.2 17.4 %shard_map.101 = (bf16[160,32,384]{2,1,0:T(8,128)(2,1)}, bf16[160,32,384]{2,1,0:T(8,128)(2,1)}) custom-call(bf16[2,320,768]{2,1,0:T(8,128)(2,1)} %reshape.434.expand_ref, bf16[2,192,6144]{2,1,0:T(8,128)(2,1)} %shard_map.87.rest_0_.a_ref, bf16[2,192,6144]{2,1,0:T(8,128)(2,1)} %collective-permute-done.18.b_ref, ...), custom_call_target="tpu_custom_call" | custom-call | flops 999999995904 | bytes 1 | tf_op jit(solution)/shard_map/pallas_call | solution.py:226
  646.8 100.9 %collective-permute-start.28 = (bf16[2,192,3072]{2,1,0:T(8,128)(2,1)}, bf16[2,192,3072]{2,1,0:T(8,128)(2,1)}, u32[]{:S(2)}, u32[]{:S(2)}) collective-permute-start(bf16[2,192,3072]{2,1,0:T(8,128)(2,1)} %shard_map.102.rest_0_.a_ref), channel_id=1, source_target_pairs={{0,2},{1,3},{6,4},{7,5},{8,10},{9,11},{14,12},{15,13},{16,18},{17,... | collective-permute-start | bytes 7077896 | tf_op jit(solution)/shard_map/ppermute | solution.py:414
  747.7 5.6 shard_map.103.rest_0_
  753.3 4.5 all-to-all-start.3
  759.1 7.8 shard_map.104.rest_0_
  769.7 10.2 shard_map.105
  781.2 23.0 %all-to-all-done.3 = bf16[160,32,384]{2,1,0:T(8,128)(2,1)} async-done(((bf16[160,32,384]{2,1,0:T(8,128)(2,1)}), bf16[160,32,384]{2,1,0:T(8,128)(2,1)}, u32[]{:S(2)}, u32[]{:S(2)}) %all-to-all-start.3) | async-done | bytes 3932192 | tf_op jit(solution)/shard_map/all_to_all | solution.py:437
  804.2 43.7 %collective-permute-done.23.away_ref = bf16[160,32,384]{2,1,0:T(8,128)(2,1)} collective-permute-done((bf16[160,32,384]{2,1,0:T(8,128)(2,1)}, bf16[160,32,384]{2,1,0:T(8,128)(2,1)}, u32[]{:S(2)}, u32[]{:S(2)}) %collective-permute-start.23) | collective-permute-done | bytes 3932192 | tf_op jit(solution)/shard_map/ppermute | solution.py:433
  847.8 5.6 shard_map.106.rest_0_
  853.4 4.5 all-to-all-start.4
  858.0 5.5 shard_map.107.rest_0_
  865.4 5.6 shard_map.108.rest_0_
  873.0 10.2 shard_map.109
  884.5 4.9 collective-permute-done.26.away_ref
  889.4 14.9 %all-to-all-done.4 = bf16[160,32,384]{2,1,0:T(8,128)(2,1)} async-done(((bf16[160,32,384]{2,1,0:T(8,128)(2,1)}), bf16[160,32,384]{2,1,0:T(8,128)(2,1)}, u32[]{:S(2)}, u32[]{:S(2)}) %all-to-all-start.4) | async-done | bytes 3932192 | tf_op jit(solution)/shard_map/all_to_all | solution.py:437
  904.3 4.1 shard_map.110.rest_0_
  908.4 4.6 all-to-all-start.5
  913.0 7.1 shard_map.111.rest_0_
  921.4 26.4 %collective-permute-done.29.away_ref = bf16[160,16,384]{2,1,0:T(8,128)(2,1)} collective-permute-done((bf16[160,16,384]{2,1,0:T(8,128)(2,1)}, bf16[160,16,384]{2,1,0:T(8,128)(2,1)}, u32[]{:S(2)}, u32[]{:S(2)}) %collective-permute-start.29) | collective-permute-done | bytes 1966112 | tf_op jit(solution)/shard_map/ppermute | solution.py:433
  947.8 4.2 shard_map.112.rest_0_
  952.0 4.3 all-to-all-start.6
  956.4 7.1 shard_map.113.near_ref.rest_0_
  963.5 24.4 %collective-permute-done.32.away_ref = bf16[160,16,384]{2,1,0:T(8,128)(2,1)} collective-permute-done((bf16[160,16,384]{2,1,0:T(8,128)(2,1)}, bf16[160,16,384]{2,1,0:T(8,128)(2,1)}, u32[]{:S(2)}, u32[]{:S(2)}) %collective-permute-start.32) | collective-permute-done | bytes 1966112 | tf_op jit(solution)/shard_map/ppermute | solution.py:433
  987.8 4.2 shard_map.114.rest_7_
  996.9 32.8 %shard_map.115.so_far_ref = f32[20,384,640]{2,1,0:T(8,128)} custom-call(bf16[20,1280,640]{2,1,0:T(8,128)(2,1)} %legendre_ref.1, bf16[4,2,20,16,384]{4,3,2,1,0:T(8,128)(2,1)} %bitcast.14.rest_1_.rest_0_, bf16[4,2,20,16,384]{4,3,2,1,0:T(8,128)(2,1)} %bitcast.16.rest_1_, bf16[4,2,20,16,384]{4,3,2,1,0:T(8,128)(2,1)} %bitcast.18.rest_1_.rest_2_, ...), custom_call_target="tpu_custom_call" | custom-call | flops 1 | bytes 1 | tf_op jit(solution)/shard_map/pallas_call | solution.py:274
  1031.0 16.0 %shard_map.116 = bf16[20,384,640]{2,1,0:T(8,128)(2,1)} custom-call(s32[20]{0:T(128)} %dynamic_slice.3.mine_ref, bf16[20,8,160,640]{3,2,1,0:T(8,128)(2,1)} %bitcast.37, f32[20,384,640]{2,1,0:T(8,128)} %shard_map.115.so_far_ref, bf16[4,2,20,16,384]{4,3,2,1,0:T(8,128)(2,1)} %bitcast.46), custom_call_target="tpu_custom_call" | custom-call | flops 1 | bytes 1 | tf_op jit(solution)/shard_map/pallas_call | solution.py:309
  (141 shorter events, 125.7 us)
Async XLA Ops:
  27.9 2.4 copy-start
  29.3 15.1 %collective-permute-start = (bf16[192,3072]{1,0:T(8,128)(2,1)S(1)}, bf16[192,3072]{1,0:T(8,128)(2,1)}, u32[]{:S(2)}, u32[]{:S(2)}) collective-permute-start(bf16[192,3072]{1,0:T(8,128)(2,1)S(1)} %slice_bitcast_fusion.7), channel_id=1, source_target_pairs={{0,1},{1,0},{2,3},{3,2},{4,5},{5,4},{6,7},{7,6},{8,9},{9,8},{10,11... | collective-permute-start | bytes 3538952 | tf_op jit(solution)/shard_map/ppermute | solution.py:412
  34.7 3.4 copy-start.12
  40.4 1.0 copy-start.5
  47.7 55.9 %collective-permute-start.1 = (bf16[2,192,3072]{2,1,0:T(8,128)(2,1)}, bf16[2,192,3072]{2,1,0:T(8,128)(2,1)S(1)}, u32[]{:S(2)}, u32[]{:S(2)}) collective-permute-start(bf16[2,192,3072]{2,1,0:T(8,128)(2,1)} %shard_map.74.rest_0_.a_ref), channel_id=1, source_target_pairs={{0,2},{1,3},{6,4},{7,5},{8,10},{9,11},{14,12},{15,13},{16,18},{17,... | collective-permute-start | bytes 7077896 | tf_op jit(solution)/shard_map/ppermute | solution.py:414
  77.5 35.3 %collective-permute-start.4 = (bf16[192,3072]{1,0:T(8,128)(2,1)}, bf16[192,3072]{1,0:T(8,128)(2,1)S(1)}, u32[]{:S(2)}, u32[]{:S(2)}) collective-permute-start(bf16[192,3072]{1,0:T(8,128)(2,1)} %slice_bitcast_fusion.5), channel_id=1, source_target_pairs={{0,1},{1,0},{2,3},{3,2},{4,5},{5,4},{6,7},{7,6},{8,9},{9,8},{10,11... | collective-permute-start | bytes 3538952 | tf_op jit(solution)/shard_map/ppermute | solution.py:412
  103.6 1.4 copy-start.3
  112.8 10.1 copy-start.1
  112.8 1.0 copy-start.10
  117.2 54.9 %collective-permute-start.6 = (bf16[2,192,3072]{2,1,0:T(8,128)(2,1)}, bf16[2,192,3072]{2,1,0:T(8,128)(2,1)}, u32[]{:S(2)}, u32[]{:S(2)}) collective-permute-start(bf16[2,192,3072]{2,1,0:T(8,128)(2,1)} %shard_map.78.rest_0_.a_ref), channel_id=1, source_target_pairs={{0,2},{1,3},{6,4},{7,5},{8,10},{9,11},{14,12},{15,13},{16,18},{17,... | collective-permute-start | bytes 7077896 | tf_op jit(solution)/shard_map/ppermute | solution.py:414
  123.0 2.9 collective-permute-start.3
  123.1 100.2 %collective-permute-start.2 = (bf16[2,320,3072]{2,1,0:T(8,128)(2,1)}, bf16[2,320,3072]{2,1,0:T(8,128)(2,1)}, u32[]{:S(2)}, u32[]{:S(2)}) collective-permute-start(bf16[2,320,3072]{2,1,0:T(8,128)(2,1)} %shard_map.77.rest_0_), channel_id=1, source_target_pairs={{2,4},{3,5},{4,2},{5,3},{10,12},{11,13},{12,10},{13,11},{18,20},{1... | collective-permute-start | bytes 11796488 | tf_op jit(solution)/shard_map/ppermute | solution.py:424
  125.9 1.0 copy-start.11
  179.9 6.9 copy-start.2
  179.9 126.8 %collective-permute-start.10 = (bf16[2,320,3072]{2,1,0:T(8,128)(2,1)}, bf16[2,320,3072]{2,1,0:T(8,128)(2,1)}, u32[]{:S(2)}, u32[]{:S(2)}) collective-permute-start(bf16[2,320,3072]{2,1,0:T(8,128)(2,1)} %shard_map.81.rest_0_), channel_id=1, source_target_pairs={{2,4},{3,5},{4,2},{5,3},{10,12},{11,13},{12,10},{13,11},{18,20},{1... | collective-permute-start | bytes 11796488 | tf_op jit(solution)/shard_map/ppermute | solution.py:424
  186.3 32.1 %collective-permute-start.5 = (bf16[192,6144]{1,0:T(8,128)(2,1)}, bf16[192,6144]{1,0:T(8,128)(2,1)}, u32[]{:S(2)}, u32[]{:S(2)}) collective-permute-start(bf16[192,6144]{1,0:T(8,128)(2,1)} %slice_bitcast_fusion.1), channel_id=1, source_target_pairs={{0,1},{1,0},{2,3},{3,2},{4,5},{5,4},{6,7},{7,6},{8,9},{9,8},{10,11... | collective-permute-start | bytes 7077896 | tf_op jit(solution)/shard_map/ppermute | solution.py:412
  186.8 56.0 %collective-permute-start.8 = (bf16[2,192,3072]{2,1,0:T(8,128)(2,1)S(1)}, bf16[2,192,3072]{2,1,0:T(8,128)(2,1)}, u32[]{:S(2)}, u32[]{:S(2)}) collective-permute-start(bf16[2,192,3072]{2,1,0:T(8,128)(2,1)S(1)} %copy-done.2), channel_id=1, source_target_pairs={{0,2},{1,3},{6,4},{7,5},{8,10},{9,11},{14,12},{15,13},{16,18},{17,... | collective-permute-start | bytes 7077896 | tf_op jit(solution)/shard_map/ppermute | solution.py:414
  198.7 1.1 copy-start.6
  250.5 115.3 %collective-permute-start.14 = (bf16[2,192,6144]{2,1,0:T(8,128)(2,1)}, bf16[2,192,6144]{2,1,0:T(8,128)(2,1)}, u32[]{:S(2)}, u32[]{:S(2)}) collective-permute-start(bf16[2,192,6144]{2,1,0:T(8,128)(2,1)} %shard_map.82.rest_0_.a_ref), channel_id=1, source_target_pairs={{0,2},{1,3},{6,4},{7,5},{8,10},{9,11},{14,12},{15,13},{16,18},{17,... | collective-permute-start | bytes 14155784 | tf_op jit(solution)/shard_map/ppermute | solution.py:414
  299.5 81.5 %collective-permute-start.13 = (bf16[2,320,3072]{2,1,0:T(8,128)(2,1)}, bf16[2,320,3072]{2,1,0:T(8,128)(2,1)}, u32[]{:S(2)}, u32[]{:S(2)}) collective-permute-start(bf16[2,320,3072]{2,1,0:T(8,128)(2,1)} %shard_map.84.rest_0_), channel_id=1, source_target_pairs={{2,4},{3,5},{4,2},{5,3},{10,12},{11,13},{12,10},{13,11},{18,20},{1... | collective-permute-start | bytes 11796488 | tf_op jit(solution)/shard_map/ppermute | solution.py:424
  305.4 11.5 %collective-permute-start.9 = (bf16[192,6144]{1,0:T(8,128)(2,1)}, bf16[192,6144]{1,0:T(8,128)(2,1)}, u32[]{:S(2)}, u32[]{:S(2)}) collective-permute-start(bf16[192,6144]{1,0:T(8,128)(2,1)} %slice_bitcast_fusion), channel_id=1, source_target_pairs={{0,1},{1,0},{2,3},{3,2},{4,5},{5,4},{6,7},{7,6},{8,9},{9,8},{10,11... | collective-permute-start | bytes 7077896 | tf_op jit(solution)/shard_map/ppermute | solution.py:412
  305.4 50.6 %collective-permute-start.7 = (bf16[160,16,384]{2,1,0:T(8,128)(2,1)}, bf16[160,16,384]{2,1,0:T(8,128)(2,1)}, u32[]{:S(2)}, u32[]{:S(2)}) collective-permute-start(bf16[160,16,384]{2,1,0:T(8,128)(2,1)} %get-tuple-element.20), channel_id=1, source_target_pairs={{2,0},{3,1},{4,6},{5,7},{10,8},{11,9},{12,14},{13,15},{18,16},{19,... | collective-permute-start | bytes 5898248 | tf_op jit(solution)/shard_map/ppermute | solution.py:433
  316.9 5.0 copy-start.8
  345.7 113.0 %collective-permute-start.18 = (bf16[2,192,6144]{2,1,0:T(8,128)(2,1)}, bf16[2,192,6144]{2,1,0:T(8,128)(2,1)}, u32[]{:S(2)}, u32[]{:S(2)}) collective-permute-start(bf16[2,192,6144]{2,1,0:T(8,128)(2,1)} %shard_map.87.rest_0_.a_ref), channel_id=1, source_target_pairs={{0,2},{1,3},{6,4},{7,5},{8,10},{9,11},{14,12},{15,13},{16,18},{17,... | collective-permute-start | bytes 14155784 | tf_op jit(solution)/shard_map/ppermute | solution.py:414
  356.0 35.1 %collective-permute-start.12 = (bf16[192,3072]{1,0:T(8,128)(2,1)}, bf16[192,3072]{1,0:T(8,128)(2,1)}, u32[]{:S(2)}, u32[]{:S(2)}) collective-permute-start(bf16[192,3072]{1,0:T(8,128)(2,1)} %slice_bitcast_fusion.4), channel_id=1, source_target_pairs={{0,1},{1,0},{2,3},{3,2},{4,5},{5,4},{6,7},{7,6},{8,9},{9,8},{10,11... | collective-permute-start | bytes 3538952 | tf_op jit(solution)/shard_map/ppermute | solution.py:412
  360.2 70.0 %all-to-all-start = ((bf16[160,16,384]{2,1,0:T(8,128)(2,1)}), bf16[160,16,384]{2,1,0:T(8,128)(2,1)}, u32[]{:S(2)}, u32[]{:S(2)}) async-start(bf16[160,16,384]{2,1,0:T(8,128)(2,1)} %shard_map.89.rest_0_), calls=%async_computation | async-start | bytes 3932160 | tf_op jit(solution)/shard_map/all_to_all | solution.py:437
  364.5 64.4 %collective-permute-start.11 = (bf16[160,16,384]{2,1,0:T(8,128)(2,1)}, bf16[160,16,384]{2,1,0:T(8,128)(2,1)}, u32[]{:S(2)}, u32[]{:S(2)}) collective-permute-start(bf16[160,16,384]{2,1,0:T(8,128)(2,1)} %get-tuple-element.22), channel_id=1, source_target_pairs={{2,0},{3,1},{4,6},{5,7},{10,8},{11,9},{12,14},{13,15},{18,16},{19,... | collective-permute-start | bytes 5898248 | tf_op jit(solution)/shard_map/ppermute | solution.py:433
  377.1 96.4 %collective-permute-start.17 = (bf16[2,320,6144]{2,1,0:T(8,128)(2,1)}, bf16[2,320,6144]{2,1,0:T(8,128)(2,1)}, u32[]{:S(2)}, u32[]{:S(2)}) collective-permute-start(bf16[2,320,6144]{2,1,0:T(8,128)(2,1)} %shard_map.90.rest_0_), channel_id=1, source_target_pairs={{2,4},{3,5},{4,2},{5,3},{10,12},{11,13},{12,10},{13,11},{18,20},{1... | collective-permute-start | bytes 23592968 | tf_op jit(solution)/shard_map/ppermute | solution.py:424
  391.1 3.6 copy-start.7
  418.4 197.3 %collective-permute-start.22 = (bf16[2,192,3072]{2,1,0:T(8,128)(2,1)}, bf16[2,192,3072]{2,1,0:T(8,128)(2,1)}, u32[]{:S(2)}, u32[]{:S(2)}) collective-permute-start(bf16[2,192,3072]{2,1,0:T(8,128)(2,1)} %shard_map.92.rest_0_.a_ref), channel_id=1, source_target_pairs={{0,2},{1,3},{6,4},{7,5},{8,10},{9,11},{14,12},{15,13},{16,18},{17,... | collective-permute-start | bytes 7077896 | tf_op jit(solution)/shard_map/ppermute | solution.py:414
  428.9 61.9 %collective-permute-start.16 = (bf16[192,3072]{1,0:T(8,128)(2,1)}, bf16[192,3072]{1,0:T(8,128)(2,1)}, u32[]{:S(2)}, u32[]{:S(2)}) collective-permute-start(bf16[192,3072]{1,0:T(8,128)(2,1)} %slice_bitcast_fusion.3), channel_id=1, source_target_pairs={{0,1},{1,0},{2,3},{3,2},{4,5},{5,4},{6,7},{7,6},{8,9},{9,8},{10,11... | collective-permute-start | bytes 3538952 | tf_op jit(solution)/shard_map/ppermute | solution.py:412
  428.9 176.6 %collective-permute-start.15 = (bf16[160,16,384]{2,1,0:T(8,128)(2,1)}, bf16[160,16,384]{2,1,0:T(8,128)(2,1)}, u32[]{:S(2)}, u32[]{:S(2)}) collective-permute-start(bf16[160,16,384]{2,1,0:T(8,128)(2,1)} %get-tuple-element.24), channel_id=1, source_target_pairs={{2,0},{3,1},{4,6},{5,7},{10,8},{11,9},{12,14},{13,15},{18,16},{19,... | collective-permute-start | bytes 5898248 | tf_op jit(solution)/shard_map/ppermute | solution.py:433
  434.3 171.2 %all-to-all-start.1 = ((bf16[160,16,384]{2,1,0:T(8,128)(2,1)}), bf16[160,16,384]{2,1,0:T(8,128)(2,1)}, u32[]{:S(2)}, u32[]{:S(2)}) async-start(bf16[160,16,384]{2,1,0:T(8,128)(2,1)} %shard_map.94.rest_0_), calls=%async_computation.1 | async-start | bytes 3932160 | tf_op jit(solution)/shard_map/all_to_all | solution.py:437
  469.7 156.5 %collective-permute-start.21 = (bf16[2,320,6144]{2,1,0:T(8,128)(2,1)}, bf16[2,320,6144]{2,1,0:T(8,128)(2,1)}, u32[]{:S(2)}, u32[]{:S(2)}) collective-permute-start(bf16[2,320,6144]{2,1,0:T(8,128)(2,1)} %shard_map.95.rest_0_), channel_id=1, source_target_pairs={{2,4},{3,5},{4,2},{5,3},{10,12},{11,13},{12,10},{13,11},{18,20},{1... | collective-permute-start | bytes 23592968 | tf_op jit(solution)/shard_map/ppermute | solution.py:424
  490.8 3.3 copy-start.9
  518.1 241.0 %collective-permute-start.25 = (bf16[2,192,3072]{2,1,0:T(8,128)(2,1)}, bf16[2,192,3072]{2,1,0:T(8,128)(2,1)}, u32[]{:S(2)}, u32[]{:S(2)}) collective-permute-start(bf16[2,192,3072]{2,1,0:T(8,128)(2,1)} %shard_map.97.rest_0_.a_ref), channel_id=1, source_target_pairs={{0,2},{1,3},{6,4},{7,5},{8,10},{9,11},{14,12},{15,13},{16,18},{17,... | collective-permute-start | bytes 7077896 | tf_op jit(solution)/shard_map/ppermute | solution.py:414
  605.5 38.1 %collective-permute-start.20 = (bf16[192,3072]{1,0:T(8,128)(2,1)}, bf16[192,3072]{1,0:T(8,128)(2,1)}, u32[]{:S(2)}, u32[]{:S(2)}) collective-permute-start(bf16[192,3072]{1,0:T(8,128)(2,1)} %slice_bitcast_fusion.2), channel_id=1, source_target_pairs={{0,1},{1,0},{2,3},{3,2},{4,5},{5,4},{6,7},{7,6},{8,9},{9,8},{10,11... | collective-permute-start | bytes 3538952 | tf_op jit(solution)/shard_map/ppermute | solution.py:412
  609.7 138.0 %all-to-all-start.2 = ((bf16[160,16,384]{2,1,0:T(8,128)(2,1)}), bf16[160,16,384]{2,1,0:T(8,128)(2,1)}, u32[]{:S(2)}, u32[]{:S(2)}) async-start(bf16[160,16,384]{2,1,0:T(8,128)(2,1)} %shard_map.99.rest_0_), calls=%async_computation.2 | async-start | bytes 3932160 | tf_op jit(solution)/shard_map/all_to_all | solution.py:437
  614.0 133.7 %collective-permute-start.19 = (bf16[160,32,384]{2,1,0:T(8,128)(2,1)}, bf16[160,32,384]{2,1,0:T(8,128)(2,1)}, u32[]{:S(2)}, u32[]{:S(2)}) collective-permute-start(bf16[160,32,384]{2,1,0:T(8,128)(2,1)} %get-tuple-element.26), channel_id=1, source_target_pairs={{2,0},{3,1},{4,6},{5,7},{10,8},{11,9},{12,14},{13,15},{18,16},{19,... | collective-permute-start | bytes 11796488 | tf_op jit(solution)/shard_map/ppermute | solution.py:433
  623.6 146.1 %collective-permute-start.24 = (bf16[2,320,3072]{2,1,0:T(8,128)(2,1)}, bf16[2,320,3072]{2,1,0:T(8,128)(2,1)}, u32[]{:S(2)}, u32[]{:S(2)}) collective-permute-start(bf16[2,320,3072]{2,1,0:T(8,128)(2,1)} %shard_map.100.rest_0_), channel_id=1, source_target_pairs={{2,4},{3,5},{4,2},{5,3},{10,12},{11,13},{12,10},{13,11},{18,20},{1... | collective-permute-start | bytes 11796488 | tf_op jit(solution)/shard_map/ppermute | solution.py:424
  646.8 211.2 %collective-permute-start.28 = (bf16[2,192,3072]{2,1,0:T(8,128)(2,1)}, bf16[2,192,3072]{2,1,0:T(8,128)(2,1)}, u32[]{:S(2)}, u32[]{:S(2)}) collective-permute-start(bf16[2,192,3072]{2,1,0:T(8,128)(2,1)} %shard_map.102.rest_0_.a_ref), channel_id=1, source_target_pairs={{0,2},{1,3},{6,4},{7,5},{8,10},{9,11},{14,12},{15,13},{16,18},{17,... | collective-permute-start | bytes 7077896 | tf_op jit(solution)/shard_map/ppermute | solution.py:414
  753.3 50.9 %all-to-all-start.3 = ((bf16[160,32,384]{2,1,0:T(8,128)(2,1)}), bf16[160,32,384]{2,1,0:T(8,128)(2,1)}, u32[]{:S(2)}, u32[]{:S(2)}) async-start(bf16[160,32,384]{2,1,0:T(8,128)(2,1)} %shard_map.103.rest_0_), calls=%async_computation.3 | async-start | bytes 7864320 | tf_op jit(solution)/shard_map/all_to_all | solution.py:437
  757.8 90.0 %collective-permute-start.23 = (bf16[160,32,384]{2,1,0:T(8,128)(2,1)}, bf16[160,32,384]{2,1,0:T(8,128)(2,1)}, u32[]{:S(2)}, u32[]{:S(2)}) collective-permute-start(bf16[160,32,384]{2,1,0:T(8,128)(2,1)} %get-tuple-element.28), channel_id=1, source_target_pairs={{2,0},{3,1},{4,6},{5,7},{10,8},{11,9},{12,14},{13,15},{18,16},{19,... | collective-permute-start | bytes 11796488 | tf_op jit(solution)/shard_map/ppermute | solution.py:433
  767.0 106.0 %collective-permute-start.27 = (bf16[2,320,3072]{2,1,0:T(8,128)(2,1)}, bf16[2,320,3072]{2,1,0:T(8,128)(2,1)}, u32[]{:S(2)}, u32[]{:S(2)}) collective-permute-start(bf16[2,320,3072]{2,1,0:T(8,128)(2,1)} %shard_map.104.rest_0_), channel_id=1, source_target_pairs={{2,4},{3,5},{4,2},{5,3},{10,12},{11,13},{12,10},{13,11},{18,20},{1... | collective-permute-start | bytes 11796488 | tf_op jit(solution)/shard_map/ppermute | solution.py:424
  779.9 109.5 %collective-permute-start.26 = (bf16[160,16,384]{2,1,0:T(8,128)(2,1)}, bf16[160,16,384]{2,1,0:T(8,128)(2,1)}, u32[]{:S(2)}, u32[]{:S(2)}) collective-permute-start(bf16[160,16,384]{2,1,0:T(8,128)(2,1)} %get-tuple-element.30), channel_id=1, source_target_pairs={{2,0},{3,1},{4,6},{5,7},{10,8},{11,9},{12,14},{13,15},{18,16},{19,... | collective-permute-start | bytes 5898248 | tf_op jit(solution)/shard_map/ppermute | solution.py:433
  853.4 50.9 %all-to-all-start.4 = ((bf16[160,32,384]{2,1,0:T(8,128)(2,1)}), bf16[160,32,384]{2,1,0:T(8,128)(2,1)}, u32[]{:S(2)}, u32[]{:S(2)}) async-start(bf16[160,32,384]{2,1,0:T(8,128)(2,1)} %shard_map.106.rest_0_), calls=%async_computation.4 | async-start | bytes 7864320 | tf_op jit(solution)/shard_map/all_to_all | solution.py:437
  863.5 49.5 %collective-permute-start.30 = (bf16[1,320,3072]{2,1,0:T(8,128)(2,1)}, bf16[1,320,3072]{2,1,0:T(8,128)(2,1)}, u32[]{:S(2)}, u32[]{:S(2)}) collective-permute-start(bf16[1,320,3072]{2,1,0:T(8,128)(2,1)} %shard_map.107.rest_0_), channel_id=1, source_target_pairs={{2,4},{3,5},{4,2},{5,3},{10,12},{11,13},{12,10},{13,11},{18,20},{1... | collective-permute-start | bytes 5898248 | tf_op jit(solution)/shard_map/ppermute | solution.py:424
  871.0 85.3 %collective-permute-start.31 = (bf16[1,320,3072]{2,1,0:T(8,128)(2,1)}, bf16[1,320,3072]{2,1,0:T(8,128)(2,1)}, u32[]{:S(2)}, u32[]{:S(2)}) collective-permute-start(bf16[1,320,3072]{2,1,0:T(8,128)(2,1)} %shard_map.108.rest_0_), channel_id=1, source_target_pairs={{2,4},{3,5},{4,2},{5,3},{10,12},{11,13},{12,10},{13,11},{18,20},{1... | collective-permute-start | bytes 5898248 | tf_op jit(solution)/shard_map/ppermute | solution.py:424
  883.2 64.6 %collective-permute-start.29 = (bf16[160,16,384]{2,1,0:T(8,128)(2,1)}, bf16[160,16,384]{2,1,0:T(8,128)(2,1)}, u32[]{:S(2)}, u32[]{:S(2)}) collective-permute-start(bf16[160,16,384]{2,1,0:T(8,128)(2,1)} %get-tuple-element.32), channel_id=1, source_target_pairs={{2,0},{3,1},{4,6},{5,7},{10,8},{11,9},{12,14},{13,15},{18,16},{19,... | collective-permute-start | bytes 5898248 | tf_op jit(solution)/shard_map/ppermute | solution.py:433
  908.4 39.4 %all-to-all-start.5 = ((bf16[160,16,384]{2,1,0:T(8,128)(2,1)}), bf16[160,16,384]{2,1,0:T(8,128)(2,1)}, u32[]{:S(2)}, u32[]{:S(2)}) async-start(bf16[160,16,384]{2,1,0:T(8,128)(2,1)} %shard_map.110.rest_0_), calls=%async_computation.5 | async-start | bytes 3932160 | tf_op jit(solution)/shard_map/all_to_all | solution.py:437
  920.1 67.7 %collective-permute-start.32 = (bf16[160,16,384]{2,1,0:T(8,128)(2,1)}, bf16[160,16,384]{2,1,0:T(8,128)(2,1)}, u32[]{:S(2)}, u32[]{:S(2)}) collective-permute-start(bf16[160,16,384]{2,1,0:T(8,128)(2,1)} %shard_map.111.rest_0_), channel_id=1, source_target_pairs={{2,0},{3,1},{4,6},{5,7},{10,8},{11,9},{12,14},{13,15},{18,16},{19,... | collective-permute-start | bytes 5898248 | tf_op jit(solution)/shard_map/ppermute | solution.py:433
  952.0 39.9 %all-to-all-start.6 = ((bf16[160,16,384]{2,1,0:T(8,128)(2,1)}), bf16[160,16,384]{2,1,0:T(8,128)(2,1)}, u32[]{:S(2)}, u32[]{:S(2)}) async-start(bf16[160,16,384]{2,1,0:T(8,128)(2,1)} %shard_map.112.rest_0_), calls=%async_computation.6 | async-start | bytes 3932160 | tf_op jit(solution)/shard_map/all_to_all | solution.py:437
  992.0 37.8 %all-to-all-start.7 = ((bf16[160,16,384]{2,1,0:T(8,128)(2,1)}), bf16[160,16,384]{2,1,0:T(8,128)(2,1)S(1)}, u32[]{:S(2)}, u32[]{:S(2)}) async-start(bf16[160,16,384]{2,1,0:T(8,128)(2,1)} %shard_map.114.rest_7_), calls=%async_computation.7 | async-start | bytes 3932160 | tf_op jit(solution)/shard_map/all_to_all | solution.py:437
  1029.7 1.3 copy-start.4
